TPU v7x, 256 devices: a whole 4x4x8 slice. The times are simulated.
256 devices in a mesh: section: 4 (over x), row: 64 (over y, z, core).
Axes of the slice: x: 4, y: 4, z: 8, core: 2. Of those that a mesh axis runs over, the one named last changes fastest.
Arguments:
- object_slices: float32 [4, 2, 1024, 1024], P('section', None, 'row'), may hold values from -5 to 5
- probe_spec: float32 [2, 1024, 1024], P(None, 'row'), may hold values from -5 to 5
- offsets: int32 [2, 2], replicated, may hold values from 0 to 1023
- measured: float32 [2, 1024, 1024], P(None, 'row'), may hold values from 0.2 to 3
Outputs:
- object_grad: float32 [4, 2, 1024, 1024], P('section', None, 'row')
All inputs are finite; a program needn't handle non-finite values.
Results may differ from a plain program's by a relative error of at most 0.0003.
Values sent between devices are 32-bit elements; how exact they have to be, the bound alone decides.
No kernel may reach another device: no remote copies, remote signals or barrier semaphores. Data moves between devices by JAX's collectives and lax.ppermute only.
A program may use at most 128 MiB of HBM per device.

v0:
```python
import math

import jax
import jax.numpy as jnp
from jax import lax
from jax.sharding import PartitionSpec as P

fresnel_coef = 0.37
highest = lax.Precision.HIGHEST


def shifted(value, axis, steps):
    count = lax.axis_size(axis)
    initial, last = (max(0, -steps), min(count, count - steps))
    return lax.ppermute(value, axis, [(source, source + steps) for source in range(initial, last)])


def complex_mul(left, right):
    return jnp.stack(
        [left[0] * right[0] - left[1] * right[1], left[0] * right[1] + left[1] * right[0]]
    )


def conj_mul(left, right):
    return jnp.stack(
        [left[0] * right[0] + left[1] * right[1], left[1] * right[0] - left[0] * right[1]]
    )


def combine_parts(result, half_len, direction):
    first = result[..., :half_len]
    second = result[..., half_len:]
    return jnp.stack([first[0] + direction * second[1], first[1] - direction * second[0]])


def small_dft(stacked, tables, direction):
    half_len = tables[0].shape[0]
    both_tables = jnp.concatenate([tables[0], tables[1]], axis=1)
    flat = stacked.reshape(-1, half_len)
    result = jnp.dot(flat, both_tables, precision=highest)
    result = result.reshape(stacked.shape[:-1] + (2 * half_len,))
    return combine_parts(result, half_len, direction)


def forward_pass(field, tables):
    half_len = tables[0].shape[0]
    halves = field.reshape(field.shape[0], field.shape[1], field.shape[2], 2, half_len)
    spectra = small_dft(halves, tables, 1.0)
    even_part = spectra[:, :, :, 0]
    turned = complex_mul(spectra[:, :, :, 1], jnp.stack([tables[2], -tables[3]]))
    joined = jnp.stack([even_part + turned, even_part - turned], axis=3)
    return joined.reshape(joined.shape[0], joined.shape[1], joined.shape[2], 2 * half_len)


def inverse_pass(field, tables):
    half_len = tables[0].shape[0]
    first_half = field[:, :, :, :half_len]
    second_half = field[:, :, :, half_len:]
    twiddle = jnp.stack([tables[2], tables[3]])
    halves = jnp.stack(
        [first_half + second_half, complex_mul(first_half - second_half, twiddle)], axis=3
    )
    spectra = small_dft(halves, tables, -1.0)
    return spectra.reshape(spectra.shape[0], spectra.shape[1], spectra.shape[2], 2 * half_len)


def forward_columns(field, tables):
    half_len = tables[0].shape[0]
    lines = field.shape[3]
    both_tables = jnp.concatenate([tables[0], tables[1]], axis=1)
    halves = field.reshape(field.shape[0], field.shape[1], 2, half_len, lines)
    result = jnp.einsum("cwajl,jk->cwalk", halves, both_tables, precision=highest)
    spectra = combine_parts(result, half_len, 1.0)
    even_part = spectra[:, :, 0]
    turned = complex_mul(spectra[:, :, 1], jnp.stack([tables[2], -tables[3]]))
    joined = jnp.stack([even_part + turned, even_part - turned], axis=3)
    return joined.reshape(joined.shape[0], joined.shape[1], lines, 2 * half_len)


def inverse_columns(field, tables):
    half_len = tables[0].shape[0]
    lines = field.shape[3]
    both_tables = jnp.concatenate([tables[0], tables[1]], axis=1)
    first_half = field[:, :, :half_len]
    second_half = field[:, :, half_len:]
    twiddle = jnp.stack([tables[2][:, None], tables[3][:, None]])
    halves = jnp.stack(
        [first_half + second_half, complex_mul(first_half - second_half, twiddle)], axis=2
    )
    result = jnp.einsum("cwajl,jk->cwlak", halves, both_tables, precision=highest)
    spectra = combine_parts(result, half_len, -1.0)
    return spectra.reshape(spectra.shape[0], spectra.shape[1], lines, 2 * half_len)


def transform_forward(field, tables):
    partial_out = forward_pass(field, tables)

    def finish(piece):
        return forward_columns(piece, tables)

    return finish(lax.all_to_all(partial_out, "row", split_axis=3, concat_axis=2, tiled=True))


def transform_inverse(field, tables):
    partial_out = inverse_pass(field, tables)

    def finish(piece):
        return inverse_columns(piece, tables)

    return finish(lax.all_to_all(partial_out, "row", split_axis=3, concat_axis=2, tiled=True))


def section_forward(spectrum, multiplier, slab_obj, tables):
    wavefield = transform_inverse(complex_mul(spectrum, multiplier), tables)
    kept = [wavefield]
    outgoing = transform_forward(complex_mul(slab_obj[0][:, None], wavefield), tables)
    return (outgoing, jnp.stack(kept))


def section_backward(adjoint, kept, multiplier, slab_obj, tables):
    layer_total = slab_obj.shape[0]
    grads = [None] * layer_total
    for layer in reversed(range(layer_total)):
        wave_adj = transform_inverse(adjoint, tables)
        grads[layer] = jnp.sum(conj_mul(wave_adj, kept[layer]), axis=1)
        field_adj = conj_mul(wave_adj, slab_obj[layer][:, None])
        backward_spec = transform_forward(field_adj, tables)
        adjoint = conj_mul(backward_spec, multiplier)
    return (adjoint, jnp.stack(grads))


def loss_adjoint(outgoing, target):
    power = outgoing[0] * outgoing[0] + outgoing[1] * outgoing[1]
    return 0.5 * (power - target)[None] * outgoing


def shards(object_slices, probe_spec, offsets, measured):
    slab_count = object_slices.shape[0]
    line_count = object_slices.shape[2]
    width = object_slices.shape[3]
    half_len = width // 2
    wave_count = offsets.shape[0]
    section_count = lax.axis_size("section")
    section_pos = lax.axis_index("section")
    row_pos = lax.axis_index("row")
    index = jnp.arange(half_len, dtype=jnp.int32)
    product = index[:, None] * index[None, :] % half_len
    angle = 2.0 * math.pi / half_len * product.astype(jnp.float32)
    scale = 1.0 / math.sqrt(width)
    twid_angle = 2.0 * math.pi / width * index.astype(jnp.float32)
    tables = (
        jnp.cos(angle) * scale,
        jnp.sin(angle) * scale,
        jnp.cos(twid_angle),
        jnp.sin(twid_angle),
    )
    column_freq = row_pos * line_count + jnp.arange(line_count, dtype=jnp.int32)
    row_freq = jnp.arange(width, dtype=jnp.int32)
    column_signed = jnp.where(column_freq < half_len, column_freq, column_freq - width)
    row_signed = jnp.where(row_freq < half_len, row_freq, row_freq - width)
    square_sum = (
        column_signed[:, None] * column_signed[:, None] + row_signed[None, :] * row_signed[None, :]
    )
    phase = -math.pi * fresnel_coef / width * square_sum.astype(jnp.float32)
    propagator = jnp.stack([jnp.cos(phase), jnp.sin(phase)])[:, None]
    turns = (
        row_freq[None, None, :] * offsets[:, 0][:, None, None]
        + column_freq[None, :, None] * offsets[:, 1][:, None, None]
    ) % width
    ramp_angle = 2.0 * math.pi / width * turns.astype(jnp.float32)
    ramps = jnp.stack([jnp.cos(ramp_angle), -jnp.sin(ramp_angle)])
    start_spec = probe_spec[:, None]
    is_first = section_pos == 0
    is_last = section_pos == section_count - 1
    group_count = wave_count // wave_count
    step_count = section_count + group_count - 1
    kept_store = jnp.zeros((slab_count, 2, wave_count, line_count, width), jnp.float32)
    far_store = jnp.zeros((2, wave_count, line_count, width), jnp.float32)
    received = jnp.zeros((2, wave_count, line_count, width), jnp.float32)
    for moment in range(step_count):
        offset_group = moment - section_pos
        active = (offset_group >= 0) & (offset_group < group_count)
        ramp_part = ramps
        multiplier = jnp.where(is_first, ramp_part, propagator)
        spectrum = jnp.where(is_first, start_spec, received)
        outgoing, kept = section_forward(spectrum, multiplier, object_slices, tables)
        kept_store = jnp.where(active, kept, kept_store)
        far_store = jnp.where(active & is_last, outgoing, far_store)
        if moment + 1 < step_count:
            received = shifted(outgoing, "section", 1)
    far_adjoint = loss_adjoint(far_store, measured)
    grads = jnp.zeros((slab_count, 2, line_count, width), jnp.float32)
    received = jnp.zeros((2, wave_count, line_count, width), jnp.float32)
    for moment in range(step_count):
        offset_group = moment - (section_count - 1 - section_pos)
        active = (offset_group >= 0) & (offset_group < group_count)
        ramp_part = ramps
        multiplier = jnp.where(is_first, ramp_part, propagator)
        adjoint = jnp.where(is_last, far_adjoint, received)
        kept = kept_store
        sent_back, grad_term = section_backward(adjoint, kept, multiplier, object_slices, tables)
        grads = grads + jnp.where(active, grad_term, 0.0)
        if moment + 1 < step_count:
            received = shifted(sent_back, "section", -1)
    return grads


def solution(mesh):
    placed = (P("section", None, "row", None), P(None, "row", None), P(), P(None, "row", None))
    return jax.shard_map(
        shards,
        mesh=mesh,
        in_specs=placed,
        out_specs=P("section", None, "row", None),
        check_vma=False,
    )
```

profile of v0, /device:TPU:1, one launch (start us, length us, event | category | flops | bytes accessed | tf_op | source)
XLA Modules:
  0.0 752.0 jit_solution(123805623323976440)
XLA Ops:
  0.1 4.2 sine_multiply_fusion
  9.4 5.0 reshape.2548
  14.4 13.4 %all-to-all-start = ((f32[64,1,1024]{2,1,0:T(1,128)}), f32[64,1,1024]{2,1,0:T(1,128)S(1)}, u32[]{:S(2)}, u32[]{:S(2)}) async-start(f32[64,1,1024]{2,1,0:T(1,128)} %reshape.2548), calls=%async_computation | async-start | bytes 524288 | tf_op jit(solution)/shard_map/all_to_all | solution.py:110
  28.1 11.6 %all-to-all-done = f32[64,1,1024]{2,1,0:T(1,128)S(1)} async-done(((f32[64,1,1024]{2,1,0:T(1,128)}), f32[64,1,1024]{2,1,0:T(1,128)S(1)}, u32[]{:S(2)}, u32[]{:S(2)}) %all-to-all-start) | async-done | bytes 262176 | tf_op jit(solution)/shard_map/all_to_all | solution.py:110
  45.5 4.2 copy.552
  58.0 4.4 reshape.2550
  62.4 17.9 %all_to_all.249 = f32[64,1,1024]{2,1,0:T(1,128)} all-to-all(f32[64,1,1024]{2,1,0:T(1,128)S(1)} %reshape.2550), channel_id=1, replica_groups=mesh['section'=4,'row'=64] {'row'}, dimensions={0} | all-to-all | bytes 524288 | tf_op jit(solution)/shard_map/all_to_all | solution.py:101
  86.6 4.2 copy.551
  98.1 5.2 collective-permute-done
  107.2 4.4 reshape.2552
  111.6 18.7 %all_to_all.250 = f32[64,1,1024]{2,1,0:T(1,128)} all-to-all(f32[64,1,1024]{2,1,0:T(1,128)S(1)} %reshape.2552), channel_id=1, replica_groups=mesh['section'=4,'row'=64] {'row'}, dimensions={0} | all-to-all | bytes 524288 | tf_op jit(solution)/shard_map/all_to_all | solution.py:110
  136.5 4.2 copy.550
  151.1 5.0 reshape.2554
  156.1 18.1 %all_to_all.251 = f32[64,1,1024]{2,1,0:T(1,128)} all-to-all(f32[64,1,1024]{2,1,0:T(1,128)} %reshape.2554), channel_id=1, replica_groups=mesh['section'=4,'row'=64] {'row'}, dimensions={0} | all-to-all | bytes 524288 | tf_op jit(solution)/shard_map/all_to_all | solution.py:101
  177.1 5.0 reshape.2555
  182.1 4.2 copy.549
  192.1 4.1 collective-permute-start.1
  196.2 5.2 collective-permute-done.1
  207.4 5.0 reshape.2556
  212.4 18.9 %all_to_all.252 = f32[64,1,1024]{2,1,0:T(1,128)} all-to-all(f32[64,1,1024]{2,1,0:T(1,128)} %reshape.2556), channel_id=1, replica_groups=mesh['section'=4,'row'=64] {'row'}, dimensions={0} | all-to-all | bytes 524288 | tf_op jit(solution)/shard_map/all_to_all | solution.py:110
  234.1 5.0 reshape.2557
  239.1 4.2 copy.548
  255.4 5.0 reshape.2558
  260.4 18.5 %all_to_all.253 = f32[64,1,1024]{2,1,0:T(1,128)} all-to-all(f32[64,1,1024]{2,1,0:T(1,128)} %reshape.2558), channel_id=1, replica_groups=mesh['section'=4,'row'=64] {'row'}, dimensions={0} | all-to-all | bytes 524288 | tf_op jit(solution)/shard_map/all_to_all | solution.py:101
  281.8 5.0 reshape.2559
  286.9 4.2 copy.547
  300.9 5.2 collective-permute-done.2
  310.0 4.4 reshape.2560
  314.4 18.7 %all_to_all.254 = f32[64,1,1024]{2,1,0:T(1,128)} all-to-all(f32[64,1,1024]{2,1,0:T(1,128)S(1)} %reshape.2560), channel_id=1, replica_groups=mesh['section'=4,'row'=64] {'row'}, dimensions={0} | all-to-all | bytes 524288 | tf_op jit(solution)/shard_map/all_to_all | solution.py:110
  339.3 4.2 copy.546
  351.8 5.0 reshape.2562
  356.8 6.4 all-to-all-start.7
  363.2 11.9 %all-to-all-done.7 = f32[64,1,1024]{2,1,0:T(1,128)} async-done(((f32[64,1,1024]{2,1,0:T(1,128)}), f32[64,1,1024]{2,1,0:T(1,128)}, u32[]{:S(2)}, u32[]{:S(2)}) %all-to-all-start.7) | async-done | bytes 262176 | tf_op jit(solution)/shard_map/all_to_all | solution.py:101
  381.4 4.2 copy.545
  396.7 5.0 reshape.2564
  401.7 18.5 %all_to_all.255 = f32[64,1,1024]{2,1,0:T(1,128)} all-to-all(f32[64,1,1024]{2,1,0:T(1,128)} %reshape.2564), channel_id=1, replica_groups=mesh['section'=4,'row'=64] {'row'}, dimensions={0} | all-to-all | bytes 524288 | tf_op jit(solution)/shard_map/all_to_all | solution.py:110
  423.0 5.0 reshape.2565
  428.1 4.2 copy.544
  445.0 5.0 reshape.2566
  450.0 18.3 %all_to_all.256 = f32[64,1,1024]{2,1,0:T(1,128)} all-to-all(f32[64,1,1024]{2,1,0:T(1,128)} %reshape.2566), channel_id=1, replica_groups=mesh['section'=4,'row'=64] {'row'}, dimensions={0} | all-to-all | bytes 524288 | tf_op jit(solution)/shard_map/all_to_all | solution.py:101
  471.2 5.0 reshape.2567
  476.2 4.2 copy.543
  487.5 9.1 %collective-permute-done.3 = f32[2,2,16,1024]{3,2,1,0:T(8,128)S(1)} collective-permute-done((f32[2,2,16,1024]{3,2,1,0:T(8,128)S(1)}, f32[2,2,16,1024]{3,2,1,0:T(8,128)S(1)}, u32[]{:S(2)}, u32[]{:S(2)}) %collective-permute-start.3) | collective-permute-done | bytes 262176 | tf_op jit(solution)/shard_map/ppermute | solution.py:15
  502.5 5.0 reshape.2568
  507.5 18.8 %all_to_all.257 = f32[64,1,1024]{2,1,0:T(1,128)} all-to-all(f32[64,1,1024]{2,1,0:T(1,128)} %reshape.2568), channel_id=1, replica_groups=mesh['section'=4,'row'=64] {'row'}, dimensions={0} | all-to-all | bytes 524288 | tf_op jit(solution)/shard_map/all_to_all | solution.py:110
  529.2 5.0 reshape.2569
  534.2 4.2 copy.542
  551.2 5.0 reshape.2570
  556.2 18.6 %all_to_all.258 = f32[64,1,1024]{2,1,0:T(1,128)} all-to-all(f32[64,1,1024]{2,1,0:T(1,128)} %reshape.2570), channel_id=1, replica_groups=mesh['section'=4,'row'=64] {'row'}, dimensions={0} | all-to-all | bytes 524288 | tf_op jit(solution)/shard_map/all_to_all | solution.py:101
  577.6 5.0 reshape.2571
  582.7 4.2 copy.541
  594.0 8.0 %collective-permute-done.4 = f32[2,2,16,1024]{3,2,1,0:T(8,128)S(1)} collective-permute-done((f32[2,2,16,1024]{3,2,1,0:T(8,128)S(1)}, f32[2,2,16,1024]{3,2,1,0:T(8,128)S(1)}, u32[]{:S(2)}, u32[]{:S(2)}) %collective-permute-start.4) | collective-permute-done | bytes 262176 | tf_op jit(solution)/shard_map/ppermute | solution.py:15
  607.9 5.0 reshape.2572
  612.9 19.1 %all_to_all.259 = f32[64,1,1024]{2,1,0:T(1,128)} all-to-all(f32[64,1,1024]{2,1,0:T(1,128)} %reshape.2572), channel_id=1, replica_groups=mesh['section'=4,'row'=64] {'row'}, dimensions={0} | all-to-all | bytes 524288 | tf_op jit(solution)/shard_map/all_to_all | solution.py:110
  634.8 5.0 reshape.2573
  639.9 4.2 copy.540
  656.8 5.0 reshape.2574
  661.8 18.1 %all_to_all.260 = f32[64,1,1024]{2,1,0:T(1,128)} all-to-all(f32[64,1,1024]{2,1,0:T(1,128)} %reshape.2574), channel_id=1, replica_groups=mesh['section'=4,'row'=64] {'row'}, dimensions={0} | all-to-all | bytes 524288 | tf_op jit(solution)/shard_map/all_to_all | solution.py:101
  682.8 5.0 reshape.2575
  687.8 4.2 copy.539
  699.1 8.0 %collective-permute-done.5 = f32[2,2,16,1024]{3,2,1,0:T(8,128)S(1)} collective-permute-done((f32[2,2,16,1024]{3,2,1,0:T(8,128)S(1)}, f32[2,2,16,1024]{3,2,1,0:T(8,128)S(1)}, u32[]{:S(2)}, u32[]{:S(2)}) %collective-permute-start.5) | collective-permute-done | bytes 262176 | tf_op jit(solution)/shard_map/ppermute | solution.py:15
  711.0 5.0 reshape.2576
  716.0 7.1 all-to-all-start.14
  742.1 4.2 copy.538
  (377 shorter events, 246.6 us)
Async XLA Ops:
  0.0 4.2 copy-start.23
  0.0 4.5 copy-start
  7.1 20.7 %copy-start.21 = (f32[1,2,16,1024]{3,2,1,0:T(8,128)S(1)}, f32[1,2,16,1024]{3,2,1,0:T(8,128)}, u32[]{:S(2)}) copy-start(f32[1,2,16,1024]{3,2,1,0:T(8,128)} %param.4) | copy-start | bytes 393220
  14.4 25.3 %all-to-all-start = ((f32[64,1,1024]{2,1,0:T(1,128)}), f32[64,1,1024]{2,1,0:T(1,128)S(1)}, u32[]{:S(2)}, u32[]{:S(2)}) async-start(f32[64,1,1024]{2,1,0:T(1,128)} %reshape.2548), calls=%async_computation | async-start | bytes 524288 | tf_op jit(solution)/shard_map/all_to_all | solution.py:110
  95.0 8.5 %copy-start.7 = (f32[2,2,2,2,8,512]{5,4,1,3,2,0:T(8,128)}, f32[2,2,2,2,8,512]{5,4,1,3,2,0:T(8,128)S(1)}, u32[]{:S(2)}) copy-start(f32[2,2,2,2,8,512]{5,4,1,3,2,0:T(8,128)S(1)} %copy.421) | copy-start | bytes 786436
  95.0 8.3 %collective-permute-start = (f32[2,2,16,1024]{3,2,1,0:T(8,128)S(1)}, f32[2,2,16,1024]{3,2,1,0:T(8,128)S(1)}, u32[]{:S(2)}, u32[]{:S(2)}) collective-permute-start(f32[2,2,16,1024]{3,2,1,0:T(8,128)S(1)} %bitcast.650), channel_id=1, source_target_pairs={{0,64},{64,128},{128,192},{1,65},{65,129},{129,193},{2,66},{66,130... | collective-permute-start | bytes 786440 | tf_op jit(solution)/shard_map/ppermute | solution.py:15
  192.1 9.5 %copy-start.9 = (f32[2,2,2,2,8,512]{5,4,1,3,2,0:T(8,128)}, f32[2,2,2,2,8,512]{5,4,1,3,2,0:T(8,128)S(1)}, u32[]{:S(2)}) copy-start(f32[2,2,2,2,8,512]{5,4,1,3,2,0:T(8,128)S(1)} %copy.424) | copy-start | bytes 786436
  192.1 9.3 %collective-permute-start.1 = (f32[2,2,16,1024]{3,2,1,0:T(8,128)S(1)}, f32[2,2,16,1024]{3,2,1,0:T(8,128)S(1)}, u32[]{:S(2)}, u32[]{:S(2)}) collective-permute-start(f32[2,2,16,1024]{3,2,1,0:T(8,128)S(1)} %bitcast.652), channel_id=1, source_target_pairs={{0,64},{64,128},{128,192},{1,65},{65,129},{129,193},{2,66},{66,130... | collective-permute-start | bytes 786440 | tf_op jit(solution)/shard_map/ppermute | solution.py:15
  249.5 1.4 copy-start.1
  296.8 9.5 %copy-start.11 = (f32[2,2,2,2,8,512]{5,4,1,3,2,0:T(8,128)}, f32[2,2,2,2,8,512]{5,4,1,3,2,0:T(8,128)S(1)}, u32[]{:S(2)}) copy-start(f32[2,2,2,2,8,512]{5,4,1,3,2,0:T(8,128)S(1)} %copy.427) | copy-start | bytes 786436
  296.8 9.3 %collective-permute-start.2 = (f32[2,2,16,1024]{3,2,1,0:T(8,128)S(1)}, f32[2,2,16,1024]{3,2,1,0:T(8,128)S(1)}, u32[]{:S(2)}, u32[]{:S(2)}) collective-permute-start(f32[2,2,16,1024]{3,2,1,0:T(8,128)S(1)} %bitcast.654), channel_id=1, source_target_pairs={{0,64},{64,128},{128,192},{1,65},{65,129},{129,193},{2,66},{66,130... | collective-permute-start | bytes 786440 | tf_op jit(solution)/shard_map/ppermute | solution.py:15
  348.0 1.4 copy-start.3
  348.0 1.4 copy-start.5
  356.8 18.4 %all-to-all-start.7 = ((f32[64,1,1024]{2,1,0:T(1,128)}), f32[64,1,1024]{2,1,0:T(1,128)}, u32[]{:S(2)}, u32[]{:S(2)}) async-start(f32[64,1,1024]{2,1,0:T(1,128)} %reshape.2562), calls=%async_computation.7 | async-start | bytes 524288 | tf_op jit(solution)/shard_map/all_to_all | solution.py:101
  389.5 1.0 copy-start.8
  389.5 1.0 copy-start.10
  389.5 1.1 copy-start.12
  389.6 1.1 copy-start.22
  486.2 10.4 %collective-permute-start.3 = (f32[2,2,16,1024]{3,2,1,0:T(8,128)S(1)}, f32[2,2,16,1024]{3,2,1,0:T(8,128)S(1)}, u32[]{:S(2)}, u32[]{:S(2)}) collective-permute-start(f32[2,2,16,1024]{3,2,1,0:T(8,128)S(1)} %pad_maximum_fusion.18), channel_id=1, source_target_pairs={{64,0},{128,64},{192,128},{65,1},{129,65},{193,129},{66,2},{130,66... | collective-permute-start | bytes 786440 | tf_op jit(solution)/shard_map/ppermute | solution.py:15
  592.7 9.3 %collective-permute-start.4 = (f32[2,2,16,1024]{3,2,1,0:T(8,128)S(1)}, f32[2,2,16,1024]{3,2,1,0:T(8,128)S(1)}, u32[]{:S(2)}, u32[]{:S(2)}) collective-permute-start(f32[2,2,16,1024]{3,2,1,0:T(8,128)S(1)} %pad_maximum_fusion.23), channel_id=1, source_target_pairs={{64,0},{128,64},{192,128},{65,1},{129,65},{193,129},{66,2},{130,66... | collective-permute-start | bytes 786440 | tf_op jit(solution)/shard_map/ppermute | solution.py:15
  697.8 9.3 %collective-permute-start.5 = (f32[2,2,16,1024]{3,2,1,0:T(8,128)S(1)}, f32[2,2,16,1024]{3,2,1,0:T(8,128)S(1)}, u32[]{:S(2)}, u32[]{:S(2)}) collective-permute-start(f32[2,2,16,1024]{3,2,1,0:T(8,128)S(1)} %pad_maximum_fusion.28), channel_id=1, source_target_pairs={{64,0},{128,64},{192,128},{65,1},{129,65},{193,129},{66,2},{130,66... | collective-permute-start | bytes 786440 | tf_op jit(solution)/shard_map/ppermute | solution.py:15
  711.0 15.7 %copy-start.2 = (f32[1,2,16,2,512]{4,2,3,1,0:T(8,128)S(1)}, f32[1,2,16,2,512]{4,2,3,1,0:T(8,128)}, u32[]{:S(2)}) copy-start(f32[1,2,16,2,512]{4,2,3,1,0:T(8,128)} %copy-done.1) | copy-start | bytes 393220
  716.0 14.9 %copy-start.6 = (f32[1,2,16,2,512]{4,2,3,1,0:T(8,128)S(1)}, f32[1,2,16,2,512]{4,2,3,1,0:T(8,128)}, u32[]{:S(2)}) copy-start(f32[1,2,16,2,512]{4,2,3,1,0:T(8,128)} %copy-done.5) | copy-start | bytes 393220
  716.0 15.7 %copy-start.4 = (f32[1,2,16,2,512]{4,2,3,1,0:T(8,128)S(1)}, f32[1,2,16,2,512]{4,2,3,1,0:T(8,128)}, u32[]{:S(2)}) copy-start(f32[1,2,16,2,512]{4,2,3,1,0:T(8,128)} %copy-done.3) | copy-start | bytes 393220
  716.0 19.8 %all-to-all-start.14 = ((f32[64,1,1024]{2,1,0:T(1,128)}), f32[64,1,1024]{2,1,0:T(1,128)}, u32[]{:S(2)}, u32[]{:S(2)}) async-start(f32[64,1,1024]{2,1,0:T(1,128)} %reshape.2576), calls=%async_computation.14 | async-start | bytes 524288 | tf_op jit(solution)/shard_map/all_to_all | solution.py:110
  725.0 9.2 %copy-start.19 = (f32[1,1,2,16,1024]{4,3,2,1,0:T(8,128)S(1)}, f32[1,1,2,16,1024]{4,3,2,1,0:T(8,128)}, u32[]{:S(2)}) copy-start(f32[1,1,2,16,1024]{4,3,2,1,0:T(8,128)} %stack.792) | copy-start | bytes 393220
  725.0 10.5 %copy-start.14 = (f32[1,2,2,2,8,512]{5,4,3,2,1,0:T(8,128)S(1)}, f32[1,2,2,2,8,512]{5,4,3,2,1,0:T(8,128)}, u32[]{:S(2)}) copy-start(f32[1,2,2,2,8,512]{5,4,3,2,1,0:T(8,128)} %get-tuple-element.28) | copy-start | bytes 393220
  725.1 9.1 %copy-start.20 = (f32[1,1,2,16,1024]{4,3,2,1,0:T(8,128)S(1)}, f32[1,1,2,16,1024]{4,3,2,1,0:T(8,128)}, u32[]{:S(2)}) copy-start(f32[1,1,2,16,1024]{4,3,2,1,0:T(8,128)} %stack.793) | copy-start | bytes 393220
  725.1 10.4 %copy-start.13 = (f32[1,2,2,2,8,512]{5,4,3,2,1,0:T(8,128)S(1)}, f32[1,2,2,2,8,512]{5,4,3,2,1,0:T(8,128)}, u32[]{:S(2)}) copy-start(f32[1,2,2,2,8,512]{5,4,3,2,1,0:T(8,128)} %get-tuple-element.27) | copy-start | bytes 393220
  725.9 9.6 %copy-start.16 = (f32[1,2,2,2,8,512]{5,4,3,2,1,0:T(8,128)S(1)}, f32[1,2,2,2,8,512]{5,4,3,2,1,0:T(8,128)}, u32[]{:S(2)}) copy-start(f32[1,2,2,2,8,512]{5,4,3,2,1,0:T(8,128)} %get-tuple-element.32) | copy-start | bytes 393220
  726.7 8.9 %copy-start.15 = (f32[1,2,2,2,8,512]{5,4,3,2,1,0:T(8,128)S(1)}, f32[1,2,2,2,8,512]{5,4,3,2,1,0:T(8,128)}, u32[]{:S(2)}) copy-start(f32[1,2,2,2,8,512]{5,4,3,2,1,0:T(8,128)} %get-tuple-element.31) | copy-start | bytes 393220
  727.4 8.1 %copy-start.18 = (f32[1,2,2,2,8,512]{5,4,3,2,1,0:T(8,128)S(1)}, f32[1,2,2,2,8,512]{5,4,3,2,1,0:T(8,128)}, u32[]{:S(2)}) copy-start(f32[1,2,2,2,8,512]{5,4,3,2,1,0:T(8,128)} %get-tuple-element.36) | copy-start | bytes 393220
  728.2 7.4 copy-start.17
where the time goes:
time: 765 us; the launch traced here: 752 us
  local copies, waits for them, and re-layouts  316 us (41%)
  blocking collectives  222 us (29%)
  waiting for transfers between devices  64.2 us (8%)
  other arithmetic  61.5 us (8%)
  matrix products  43.2 us (6%)
  starting transfers between devices  42.2 us (6%)
    unnamed x78, local copies, waits for them, and re-layouts  144 us
    all_to_all x6, blocking collectives, transform_inverse(): lax.all_to_all(partial_out, 'row', split_axis=3, concat_axis=2, tiled=True)  113 us
    all_to_all x6, blocking collectives, transform_forward(): lax.all_to_all(partial_out, 'row', split_axis=3, concat_axis=2, tiled=True)  110 us
    all_to_all x17, local copies, waits for them, and re-layouts, transform_inverse(): lax.all_to_all(partial_out, 'row', split_axis=3, concat_axis=2, tiled=True)  61.9 us
    ppermute x6, waiting for transfers between devices, shifted(): lax.ppermute(value, axis, [(source, source + steps) for source in range(i...  40.7 us
    another operation x32, local copies, waits for them, and re-layouts, combine_parts(): jnp.stack([first[0] + direction * second[1], first[1] - direction * secon...  32.3 us
    all_to_all x7, local copies, waits for them, and re-layouts, transform_forward(): lax.all_to_all(partial_out, 'row', split_axis=3, concat_axis=2, tiled=True)  29.2 us
    reshape x7, local copies, waits for them, and re-layouts, forward_pass(): joined.reshape(joined.shape[0], joined.shape[1], joined.shape[2], 2 * hal...  23.1 us
  transfers between devices with their start and end apart: 9, of which 8 were waited for; matrix products, arithmetic and copies ran while one was open for 2% of the time, Pallas kernels for 0%

commit v1 on v0

v1 whole, which is shorter than its diff:
```python
import math

import jax
import jax.numpy as jnp
import numpy as np
from jax import lax
from jax.experimental import pallas as pl
from jax.experimental.pallas import tpu as pltpu
from jax.sharding import PartitionSpec as P


N = 1024
B = 64
T = 16
L = T * T
fresnel_coef = 0.37
f32 = jnp.float32
bf16 = jnp.bfloat16


def split2(value):
    high = value.astype(bf16)
    return high, (value - high.astype(f32)).astype(bf16)


def np_split2(table):
    table = np.asarray(table, np.float64).astype(np.float32)
    high = table.astype(bf16)
    low = (table - high.astype(np.float32)).astype(bf16)
    return high, low


def left_table(cosine, sine):
    both = np.concatenate([cosine, sine], axis=0)
    high, low = np_split2(both)
    return np.concatenate([high, low, high], axis=1)


def pair(angle, scale=1.0):
    return np.stack([np.cos(angle), np.sin(angle)]).astype(np.float32) * np.float32(scale)


def complex_matrix(angle, scale):
    cosine, sine = np.cos(angle) * scale, np.sin(angle) * scale
    return np.concatenate(
        [np.concatenate([cosine, -sine], axis=1), np.concatenate([sine, cosine], axis=1)], axis=0
    )


def make_tables():
    two_pi = 2.0 * math.pi
    r32 = np.arange(32)
    r16 = np.arange(16)
    r8 = np.arange(8)
    blocks = np.arange(B)
    hb, ab = blocks // 32, blocks % 32
    lane_v, lane_t = np.repeat(r16, 16), np.tile(r16, 16)
    tab = {}
    angle = two_pi * np.outer(r32, r32) / 32
    eye2 = np.eye(2)
    tab["ly"] = left_table(np.kron(eye2, np.cos(angle)) / 8, np.kron(eye2, np.sin(angle)) / 8)
    tab["ty"] = pair(two_pi * (2 * lane_t[None, :] + hb[:, None]) * ab[:, None] / N)
    small = two_pi * np.outer(r16, r16) / 16
    mat = complex_matrix(small, 0.25)
    mat = mat.reshape(2, 16, 2, 16)
    full = np.einsum("atbk,vw->avtbwk", mat, np.eye(8)).reshape(256, 256)
    tab["ry"] = np.stack(np_split2(full))
    half = np.broadcast_to(two_pi * lane_t[None, :] / 32, (8, L))
    tab["by"] = pair(half)
    tab["by0"] = pair(np.broadcast_to(two_pi * lane_v[None, :] / 32, (8, L)))
    q = 2 * ab + hb
    angle = two_pi * np.outer(blocks, q) / B
    tab["lxf"] = left_table(np.cos(angle) / 8, np.sin(angle) / 8)
    tab["lxi"] = left_table(np.cos(angle.T) / 8, np.sin(angle.T) / 8)
    place = lane_v // 8 + 2 * (lane_v % 8)
    tab["tx"] = pair(two_pi * q[:, None] * place[None, :] / N)
    mat = complex_matrix(two_pi * np.outer(r8, r8) / 8, 0.25).reshape(2, 8, 2, 8)
    full = np.einsum("avbw,ts->avtbws", mat, np.eye(16)).reshape(256, 256)
    tab["rx"] = np.stack(np_split2(full))
    tab["bx"] = pair(np.broadcast_to(two_pi * np.repeat(r8, 16)[None, :] / 16, (8, 128)))
    signed = lambda freq: np.where(freq < N // 2, freq, freq - N).astype(np.float64)
    ky = ab[:, None] + 32 * lane_t[None, :] + 512 * hb[:, None]
    kx = 16 * blocks[:, None] + place[None, :]
    tab["hy"] = pair(-math.pi * fresnel_coef / N * signed(ky) ** 2)
    tab["hx"] = pair(-math.pi * fresnel_coef / N * signed(kx) ** 2)
    mat = complex_matrix(-small, 0.25).reshape(2, 16, 2, 16)
    order = np.zeros((16, 16))
    spot = np.arange(16)
    order[spot // 8 + 2 * (spot % 8), spot] = 1.0
    full = np.einsum("akbt,uw->akubwt", mat, order).reshape(512, 512)
    tab["ry0"] = np.stack(np_split2(full))
    tab["pm"] = np.einsum("kl,uw->kuwl", np.eye(16), order).reshape(256, 256).astype(bf16)
    return tab


TAB = make_tables()


def mul(a, t):
    return a[0] * t[0] - a[1] * t[1], a[0] * t[1] + a[1] * t[0]


def mul_conj(a, t):
    return a[0] * t[0] + a[1] * t[1], a[1] * t[0] - a[0] * t[1]


def left(table, a, sign):
    high, low = split2(jnp.concatenate(a, axis=1))
    stacked = jnp.concatenate([high, high, low], axis=0)
    out = jnp.dot(table, stacked, preferred_element_type=f32)
    c_re, c_im, s_re, s_im = out[:B, :L], out[:B, L:], out[B:, :L], out[B:, L:]
    if sign > 0:
        return c_re + s_im, c_im - s_re
    return c_re - s_im, c_im + s_re


def times(data, table):
    rows = data.shape[0]
    high, low = split2(data)
    out = jnp.dot(jnp.concatenate([high, low], axis=0), table[0], preferred_element_type=f32)
    return out[:rows] + out[rows:] + jnp.dot(high, table[1], preferred_element_type=f32)


def right(table, a, sign):
    re, im = a
    if sign < 0:
        im = -im
    stacked = jnp.concatenate(
        [
            jnp.concatenate([re[:, :128], im[:, :128]], axis=1),
            jnp.concatenate([re[:, 128:], im[:, 128:]], axis=1),
        ],
        axis=0,
    )
    out = times(stacked, table)
    re = jnp.concatenate([out[:B, :128], out[B:, :128]], axis=1)
    im = jnp.concatenate([out[:B, 128:], out[B:, 128:]], axis=1)
    return (re, im) if sign > 0 else (re, -im)


def rows_join(a, b):
    return tuple(jnp.concatenate([x, y], axis=0) for x, y in zip(a, b))


def lanes_join(a, b):
    return tuple(jnp.concatenate([x, y], axis=1) for x, y in zip(a, b))


def plus(a, b):
    return a[0] + b[0], a[1] + b[1]


def minus(a, b):
    return a[0] - b[0], a[1] - b[1]


def y_forward(a, tab):
    a = left(tab["ly"], a, 1)
    a = mul_conj(a, tab["ty"])
    a = right(tab["ry"], a, 1)
    first = tuple(x[:32] for x in a)
    second = mul_conj(tuple(x[32:] for x in a), tuple(x[:1] for x in tab["by"]))
    return rows_join(plus(first, second), minus(first, second))


def y_unfold(a, turn):
    first, second = tuple(x[:32] for x in a), tuple(x[32:] for x in a)
    return plus(first, second), mul(minus(first, second), tuple(x[:1] for x in turn))


def y_inverse(a, tab):
    a = right(tab["ry"], rows_join(*y_unfold(a, tab["by"])), -1)
    a = mul(a, tab["ty"])
    return left(tab["ly"], a, -1)


def x_forward(a, tab):
    first, second = tuple(x[:, :128] for x in a), tuple(x[:, 128:] for x in a)
    turned = mul_conj(minus(first, second), tuple(x[:1] for x in tab["bx"]))
    a = right(tab["rx"], lanes_join(plus(first, second), turned), 1)
    a = mul_conj(a, tab["tx"])
    return left(tab["lxf"], a, 1)


def x_inverse(a, tab):
    a = left(tab["lxi"], a, -1)
    a = mul(a, tab["tx"])
    a = right(tab["rx"], a, -1)
    first = tuple(x[:, :128] for x in a)
    second = mul(tuple(x[:, 128:] for x in a), tuple(x[:1] for x in tab["bx"]))
    return lanes_join(plus(first, second), minus(first, second))


def spread(block):
    turned = block.T
    halves = [
        jnp.concatenate([turned[base + 32 * v : base + 32 * v + 32] for v in range(T)], axis=1)
        for base in (0, 512)
    ]
    return jnp.concatenate(halves, axis=0)


def collect(block):
    parts = [
        block[32 * h : 32 * h + 32, T * v : T * v + T] for h in range(2) for v in range(T)
    ]
    return jnp.concatenate(parts, axis=0).T


Y_TABLES = ("ly", "ty", "ry", "by", "hy")
X_TABLES = ("lxf", "lxi", "tx", "rx", "bx", "hx")


def parts_of(value, at=0):
    return value[:, at : at + L], value[:, at + L : at + 2 * L]


def first_math(tab, obj, probe, target, dy, dx, row_pos):
    lanes = lax.broadcasted_iota(jnp.int32, (8, N), 1)
    which = lax.broadcasted_iota(jnp.int32, (8, N), 0)
    turns = (lanes * dy - 256 * which) & (N - 1)
    wave = jnp.cos(turns.astype(f32) * f32(2.0 * math.pi / N))
    cos_y, sin_y = wave[0:1], wave[1:2]
    kx = lax.broadcasted_iota(jnp.int32, (T, 128), 0) + row_pos * T
    lane = lax.broadcasted_iota(jnp.int32, (T, 128), 1)
    turns = (kx * dx - 256 * lane) & (N - 1)
    wave = jnp.cos(turns.astype(f32) * f32(2.0 * math.pi / N))
    cos_x, sin_x = wave[:, 0:1], wave[:, 1:2]
    ramp = (cos_y * cos_x - sin_y * sin_x, cos_y * sin_x + sin_y * cos_x)
    shifted = mul_conj(probe, ramp)
    spec = tuple(spread(x) for x in shifted)
    spec = rows_join(*y_unfold(spec, tab["by0"]))
    out = times(jnp.concatenate(spec, axis=1), tab["ry0"])
    field = left(tab["ly"], mul((out[:, :L], out[:, L:]), tab["ty"]), -1)
    target = spread(target)
    high, rest = split2(target)
    left_over = target - high.astype(f32)
    middle = left_over.astype(bf16)
    lowest = (left_over - middle.astype(f32)).astype(bf16)
    moved = jnp.dot(
        jnp.concatenate([high, middle, lowest], axis=0), tab["pm"], preferred_element_type=f32
    )
    target = moved[:B] + (moved[B : 2 * B] + moved[2 * B :])
    planes = tuple(spread(x) for x in obj)
    return jnp.concatenate(field + (target,) + planes, axis=1), jnp.concatenate(planes, axis=1)


def forward_of(axis):
    return y_forward if axis == "y" else x_forward


def inverse_of(axis):
    return y_inverse if axis == "y" else x_inverse


def propagate(axis, a, tab, conj):
    spec = forward_of(axis)(a, tab)
    times_h = mul_conj if conj else mul
    return inverse_of(axis)(times_h(spec, tab["h" + axis]), tab)


def pick(own, others, pos, home):
    out = own
    for step, value in enumerate(others, start=1):
        out = jnp.where((pos - home) % 4 == step, value, out)
    return out


VMEM_LIMIT = 40 * 1024 * 1024


def call(body, names, operands, out_shapes, scalars=()):
    tables = [jnp.asarray(TAB[name]) for name in names]
    smem = len(scalars)
    count = smem + len(operands)

    def kernel(*refs):
        scalar_refs = refs[:smem]
        ins = refs[smem:count]
        table_refs = refs[count : count + len(names)]
        outs = refs[count + len(names) :]
        tab = {}
        for name, ref in zip(names, table_refs):
            if name in ("ly", "lxf", "lxi", "pm"):
                tab[name] = ref[...]
            else:
                tab[name] = (ref[0], ref[1])
        body(tab, scalar_refs, ins, outs)

    return pl.pallas_call(
        kernel,
        out_shape=[jax.ShapeDtypeStruct(shape, f32) for shape in out_shapes],
        in_specs=[pl.BlockSpec(memory_space=pltpu.SMEM)] * smem
        + [pl.BlockSpec(memory_space=pltpu.VMEM)] * (len(operands) + len(names)),
        out_specs=[pl.BlockSpec(memory_space=pltpu.VMEM)] * len(out_shapes),
        compiler_params=pltpu.CompilerParams(vmem_limit_bytes=VMEM_LIMIT),
    )(*scalars, *operands, *tables)


def exchange(value):
    return lax.all_to_all(value, "row", split_axis=0, concat_axis=0, tiled=True)


def shards(object_slices, probe_spec, offsets, measured):
    def spread_slices(value, homes):
        return [
            lax.ppermute(value, "section", [(home, (home + step) % 4) for home in homes])
            for step in (1, 2, 3)
        ]

    def first(tab, scalars, ins, outs):
        wave = lax.axis_index("section") % 2
        row_pos = lax.axis_index("row")
        obj, probe, target = ins
        sent, planes = first_math(
            tab,
            (obj[0, 0], obj[0, 1]),
            (probe[0], probe[1]),
            jnp.where(wave == 0, target[0], target[1]),
            scalars[0][wave, 0],
            scalars[0][wave, 1],
            row_pos,
        )
        outs[0][...] = sent
        outs[1][...] = planes

    sent, planes = call(
        first,
        ("ly", "ty", "by0", "ry0", "pm"),
        (object_slices, probe_spec, measured),
        ((B, 5 * L), (B, 2 * L)),
        scalars=(offsets,),
    )
    row_objects = spread_slices(planes, (0, 2))
    got = exchange(sent)

    def chosen(ins, home):
        pos = lax.axis_index("section")
        return parts_of(pick(ins[0], ins[1:], pos, home))

    def second(tab, scalars, ins, outs):
        value = ins[0][...]
        psi = x_inverse(parts_of(value), tab)
        outs[0][...] = jnp.concatenate(psi, axis=1)
        obj = chosen([ref[...] for ref in ins[1:]], 0)
        a = propagate("x", mul(psi, obj), tab, False)
        outs[1][...] = jnp.concatenate(a, axis=1)
        outs[2][...] = value[:, 3 * L :]
        outs[3][...] = value[:, 2 * L : 3 * L]

    psi0, sent, columns, target = call(
        second,
        X_TABLES,
        (got, planes, *row_objects),
        ((B, 2 * L), (B, 2 * L), (B, 2 * L), (B, L)),
    )
    column_objects = spread_slices(columns, (1, 3))
    row_all = (planes, *row_objects)
    column_all = (columns, *column_objects)

    def inner(axis, home, last):
        def body(tab, scalars, ins, outs):
            psi = propagate(axis, parts_of(ins[0][...]), tab, False)
            outs[0][...] = jnp.concatenate(psi, axis=1)
            a = mul(psi, chosen([ref[...] for ref in ins[1:]], home))
            a = y_forward(a, tab) if last else propagate(axis, a, tab, False)
            outs[1][...] = jnp.concatenate(a, axis=1)

        return body

    square = ((B, 2 * L), (B, 2 * L))
    psi1, sent = call(inner("y", 1, False), Y_TABLES, (exchange(sent), *column_all), square)
    psi2, sent = call(inner("x", 2, False), X_TABLES, (exchange(sent), *row_all), square)
    psi3, sent = call(inner("y", 3, True), Y_TABLES, (exchange(sent), *column_all), square)

    def far(tab, scalars, ins, outs):
        phi = x_forward(parts_of(ins[0][...]), tab)
        weight = 0.5 * (phi[0] * phi[0] + phi[1] * phi[1] - ins[1][...])
        a = x_inverse((phi[0] * weight, phi[1] * weight), tab)
        outs[0][...] = jnp.concatenate(a, axis=1)

    (sent,) = call(far, X_TABLES, (exchange(sent), target), ((B, 2 * L),))

    def back(axis, home, top, both):
        def body(tab, scalars, ins, outs):
            a = parts_of(ins[0][...])
            adj = y_inverse(a, tab) if top else propagate(axis, a, tab, True)
            grad = mul_conj(adj, parts_of(ins[1][...]))
            a = mul_conj(adj, chosen([ref[...] for ref in ins[2:]], home))
            a = propagate(axis, a, tab, True)
            if both:
                outs[0][...] = jnp.concatenate(a + grad, axis=1)
            else:
                outs[0][...] = jnp.concatenate(a, axis=1)
                outs[1][...] = jnp.concatenate(grad, axis=1)

        return body

    wide = ((B, 4 * L),)
    (sent,) = call(back("y", 3, True, True), Y_TABLES, (exchange(sent), psi3, *column_all), wide)
    got3 = exchange(sent)
    sent, grad2 = call(back("x", 2, False, False), X_TABLES, (got3, psi2, *row_all), square)
    (sent,) = call(back("y", 1, False, True), Y_TABLES, (exchange(sent), psi1, *column_all), wide)
    got1 = exchange(sent)

    def final(tab, scalars, ins, outs):
        adj = propagate("x", parts_of(ins[0][...]), tab, True)
        grad0 = mul_conj(adj, parts_of(ins[1][...]))
        grads = (
            grad0,
            parts_of(ins[0][...], 2 * L),
            parts_of(ins[2][...]),
            parts_of(ins[3][...], 2 * L),
        )
        pos = lax.axis_index("section")
        for out, target_pos in ((outs[0], pos), (outs[1], pos + 1 - 2 * (pos % 2))):
            for part in range(2):
                value = grads[0][part]
                for layer in (1, 2, 3):
                    value = jnp.where(target_pos == layer, grads[layer][part], value)
                out[part] = collect(value)

    kept, given = call(
        final,
        X_TABLES,
        (got1, psi0, grad2, got3),
        ((2, T, N), (2, T, N)),
    )
    taken = lax.ppermute(given, "section", [(0, 1), (1, 0), (2, 3), (3, 2)])
    return (kept + taken)[None]


def solution(mesh):
    placed = (P("section", None, "row", None), P(None, "row", None), P(), P(None, "row", None))
    return jax.shard_map(
        shards,
        mesh=mesh,
        in_specs=placed,
        out_specs=P("section", None, "row", None),
        check_vma=False,
    )
```

time: 765 us -> 200 us (0.26); the launches traced: 752 us -> 199 us
  local copies, waits for them, and re-layouts: 316 us -> 11.3 us
  blocking collectives: 222 us -> 116 us
  other arithmetic: 61.5 us -> 0.67 us
  waiting for transfers between devices: 64.2 us -> 18 us
  matrix products: 43.2 us -> 0 us
  Pallas kernels: 0 us -> 15.5 us
    unnamed x78 -> x49, local copies, waits for them, and re-layouts: 144 us -> 8.22 us
    all_to_all x12 -> x7, blocking collectives: 222 us -> 116 us  [exchange(): return lax.all_to_all(value, 'row', split_axis=0, concat_axis=0, tiled=True)]
    all_to_all x24 -> x9, local copies, waits for them, and re-layouts: 91 us -> 3.07 us  [exchange(): return lax.all_to_all(value, 'row', split_axis=0, concat_axis=0, tiled=True)]
    reshape x18 -> x0, local copies, waits for them, and re-layouts: 45.1 us -> none  [the longest x7 23.1 us: forward_pass(): joined.reshape(joined.shape[0], joined.shape[1], joined.shape[2], 2 * hal...]
    dot_general x30 -> x0, matrix products: 43.2 us -> none  [the longest x15 19.2 us: small_dft(): result = jnp.dot(flat, both_tables, precision=highest)]
    all_to_all x15 -> x0, other arithmetic: 37.6 us -> none  [the longest x8 19.1 us: transform_inverse(): lax.all_to_all(partial_out, 'row', split_axis=3, concat_axis=2, tiled=True)]
    ppermute x6 -> x7, waiting for transfers between devices: 40.7 us -> 6.18 us  [the longest x1 4.61 us: shards(): taken = lax.ppermute(given, 'section', [(0, 1), (1, 0), (2, 3), (3, 2)])]
    another operation x32 -> x0, local copies, waits for them, and re-layouts: 32.3 us -> none  [combine_parts(): jnp.stack([first[0] + direction * second[1], first[1] - direction * secon...]
  transfers between devices with their start and end apart: 9 -> 9, of which waited for: 8 -> 4; matrix products, arithmetic and copies ran while one was open for 2% -> 0% of each run, Pallas kernels for 0% -> 0%
where the time goes in v1:
time: 200 us; the launch traced here: 199 us
  blocking collectives  116 us (58%)
  starting transfers between devices  36.8 us (18%)
  waiting for transfers between devices  18 us (9%)
  Pallas kernels  15.5 us (8%)
  local copies, waits for them, and re-layouts  11.3 us (6%)
    all_to_all x7, blocking collectives, exchange(): return lax.all_to_all(value, 'row', split_axis=0, concat_axis=0, tiled=True)  116 us
    all_to_all x2, starting transfers between devices, exchange(): return lax.all_to_all(value, 'row', split_axis=0, concat_axis=0, tiled=True)  25.1 us
    pallas_call x10, Pallas kernels, call(): pl.pallas_call(kernel, out_shape=[jax.ShapeDtypeStruct(shape, f32) for sh...  15.5 us
    all_to_all x2, waiting for transfers between devices, exchange(): return lax.all_to_all(value, 'row', split_axis=0, concat_axis=0, tiled=True)  11.9 us
    ppermute x6, starting transfers between devices, spread_slices(): lax.ppermute(value, 'section', [(home, (home + step) % 4) for home in hom...  11.6 us
    unnamed x49, local copies, waits for them, and re-layouts  8.22 us
    ppermute x1, waiting for transfers between devices, shards(): taken = lax.ppermute(given, 'section', [(0, 1), (1, 0), (2, 3), (3, 2)])  4.61 us
  transfers between devices with their start and end apart: 9, of which 4 were waited for; matrix products, arithmetic and copies ran while one was open for 0% of the time, Pallas kernels for 0%

profile of v1, /device:TPU:1, one launch (start us, length us, event | category | flops | bytes accessed | tf_op | source)
XLA Modules:
  0.0 199.1 jit_solution(14305808071062882160)
XLA Ops:
  0.0 0.7 copy-done.18
  0.7 0.9 copy-done.2
  1.6 0.8 copy-done.7
  2.5 1.2 copy-done.11
  3.7 0.9 copy-done.14
  4.6 0.9 copy-done.15
  5.5 0.9 copy-done.16
  6.4 0.9 copy-done.17
  7.3 0.7 copy-done.19
  8.0 2.2 %shard_map.172 = (f32[64,1280]{1,0:T(8,128)S(1)}, f32[64,512]{1,0:T(8,128)S(1)}) custom-call(s32[2,2]{1,0:T(2,128)S(1)} %copy-done.19, f32[1,2,16,1024]{3,2,1,0:T(8,128)S(1)} %copy-done.14, f32[2,16,1024]{2,1,0:T(8,128)S(1)} %copy-done.15, f32[2,16,1024]{2,1,0:T(8,128)S(1)} %copy-done.16, bf16[128,192]{1,0:T(8,128)(2,1)S(1)} %copy-done.7, ...), custom_call_target="tpu_custom_call" | custom-call | tf_op jit(solution)/shard_map/pallas_call | solution.py:290
  10.2 1.1 copy.19
  11.2 13.3 %all-to-all-start = ((f32[64,1,1280]{2,1,0:T(1,128)}), f32[64,1,1280]{2,1,0:T(1,128)S(1)}, u32[]{:S(2)}, u32[]{:S(2)}) async-start(f32[64,1,1280]{2,1,0:T(1,128)} %copy.19), calls=%async_computation | async-start | bytes 655360 | tf_op jit(solution)/shard_map/all_to_all | solution.py:301
  24.5 0.0 copy-start
  24.5 0.0 copy-start.4
  24.5 0.0 copy-start.5
  24.6 0.0 copy-start.9
  24.6 0.0 copy-start.10
  24.6 4.5 %collective-permute-start.2 = (f32[64,512]{1,0:T(8,128)S(1)}, f32[64,512]{1,0:T(8,128)S(1)}, u32[]{:S(2)}, u32[]{:S(2)}) collective-permute-start(f32[64,512]{1,0:T(8,128)S(1)} %get-tuple-element.22.refs_1_.refs_2_), channel_id=1, source_target_pairs={{0,192},{128,64},{1,193},{129,65},{2,194},{130,66},{3,195},{131,67... | collective-permute-start | bytes 393224 | tf_op jit(solution)/shard_map/ppermute | solution.py:307
  29.1 2.4 %collective-permute-start.1 = (f32[64,512]{1,0:T(8,128)S(1)}, f32[64,512]{1,0:T(8,128)S(1)}, u32[]{:S(2)}, u32[]{:S(2)}) collective-permute-start(f32[64,512]{1,0:T(8,128)S(1)} %get-tuple-element.22.refs_1_.refs_2_), channel_id=1, source_target_pairs={{0,128},{128,0},{1,129},{129,1},{2,130},{130,2},{3,131},{131,3},{4... | collective-permute-start | bytes 393224 | tf_op jit(solution)/shard_map/ppermute | solution.py:307
  31.5 1.3 collective-permute-start
  32.9 4.9 %all-to-all-done = f32[64,1,1280]{2,1,0:T(1,128)S(1)} async-done(((f32[64,1,1280]{2,1,0:T(1,128)}), f32[64,1,1280]{2,1,0:T(1,128)S(1)}, u32[]{:S(2)}, u32[]{:S(2)}) %all-to-all-start) | async-done | bytes 327712 | tf_op jit(solution)/shard_map/all_to_all | solution.py:301
  37.8 0.0 collective-permute-done.2.refs_4_.refs_5_
  37.8 0.0 collective-permute-done.1.refs_3_.refs_4_
  37.8 0.0 collective-permute-done.refs_2_.refs_3_
  37.9 1.3 shard_map.173
  39.2 0.0 copy-start.8
  39.2 0.0 copy-start.12
  39.2 0.8 copy.20
  40.0 11.8 %all-to-all-start.1 = ((f32[64,1,512]{2,1,0:T(1,128)}), f32[64,1,512]{2,1,0:T(1,128)S(1)}, u32[]{:S(2)}, u32[]{:S(2)}) async-start(f32[64,1,512]{2,1,0:T(1,128)} %copy.20), calls=%async_computation.1 | async-start | bytes 262144 | tf_op jit(solution)/shard_map/all_to_all | solution.py:301
  51.8 0.0 copy-start.3
  51.8 0.0 copy-start.6
  51.8 1.4 collective-permute-start.5
  53.2 0.7 collective-permute-start.4
  53.9 1.3 collective-permute-start.3
  55.2 6.9 %all-to-all-done.1 = f32[64,1,512]{2,1,0:T(1,128)S(1)} async-done(((f32[64,1,512]{2,1,0:T(1,128)}), f32[64,1,512]{2,1,0:T(1,128)S(1)}, u32[]{:S(2)}, u32[]{:S(2)}) %all-to-all-start.1) | async-done | bytes 131104 | tf_op jit(solution)/shard_map/all_to_all | solution.py:301
  62.2 0.0 collective-permute-done.5.refs_4_.refs_5_
  62.2 0.0 collective-permute-done.4.refs_3_.refs_4_
  62.2 1.6 collective-permute-done.3.refs_2_.refs_3_
  63.7 0.0 copy-done.1
  63.8 1.7 shard_map.174
  65.4 0.1 copy.21
  65.6 21.7 %all_to_all.99 = f32[64,1,512]{2,1,0:T(1,128)S(1)} all-to-all(f32[64,1,512]{2,1,0:T(1,128)S(1)} %copy.21), channel_id=1, replica_groups=mesh['section'=4,'row'=64] {'row'}, dimensions={0} | all-to-all | bytes 262144 | tf_op jit(solution)/shard_map/all_to_all | solution.py:301
  87.3 1.7 shard_map.175
  89.0 0.1 copy.22
  89.2 15.0 %all_to_all.100 = f32[64,1,512]{2,1,0:T(1,128)S(1)} all-to-all(f32[64,1,512]{2,1,0:T(1,128)S(1)} %copy.22), channel_id=1, replica_groups=mesh['section'=4,'row'=64] {'row'}, dimensions={0} | all-to-all | bytes 262144 | tf_op jit(solution)/shard_map/all_to_all | solution.py:301
  104.2 1.2 shard_map.176
  105.5 0.1 copy.23
  105.6 15.0 %all_to_all.101 = f32[64,1,512]{2,1,0:T(1,128)S(1)} all-to-all(f32[64,1,512]{2,1,0:T(1,128)S(1)} %copy.23), channel_id=1, replica_groups=mesh['section'=4,'row'=64] {'row'}, dimensions={0} | all-to-all | bytes 262144 | tf_op jit(solution)/shard_map/all_to_all | solution.py:301
  120.7 0.9 shard_map.177
  121.6 0.1 copy.24
  121.7 15.0 %all_to_all.102 = f32[64,1,512]{2,1,0:T(1,128)S(1)} all-to-all(f32[64,1,512]{2,1,0:T(1,128)S(1)} %copy.24), channel_id=1, replica_groups=mesh['section'=4,'row'=64] {'row'}, dimensions={0} | all-to-all | bytes 262144 | tf_op jit(solution)/shard_map/all_to_all | solution.py:301
  136.8 1.3 shard_map.178
  138.0 0.3 copy.25
  138.3 16.7 %all_to_all.103 = f32[64,1,1024]{2,1,0:T(1,128)S(1)} all-to-all(f32[64,1,1024]{2,1,0:T(1,128)S(1)} %copy.25), channel_id=1, replica_groups=mesh['section'=4,'row'=64] {'row'}, dimensions={0} | all-to-all | bytes 524288 | tf_op jit(solution)/shard_map/all_to_all | solution.py:301
  155.1 1.7 shard_map.179
  156.8 0.1 copy.26
  156.9 16.2 %all_to_all.104 = f32[64,1,512]{2,1,0:T(1,128)S(1)} all-to-all(f32[64,1,512]{2,1,0:T(1,128)S(1)} %copy.26), channel_id=1, replica_groups=mesh['section'=4,'row'=64] {'row'}, dimensions={0} | all-to-all | bytes 262144 | tf_op jit(solution)/shard_map/all_to_all | solution.py:301
  173.1 1.7 shard_map.180
  174.8 0.3 copy.27
  175.1 16.7 %all_to_all.105 = f32[64,1,1024]{2,1,0:T(1,128)S(1)} all-to-all(f32[64,1,1024]{2,1,0:T(1,128)S(1)} %copy.27), channel_id=1, replica_groups=mesh['section'=4,'row'=64] {'row'}, dimensions={0} | all-to-all | bytes 524288 | tf_op jit(solution)/shard_map/all_to_all | solution.py:301
  191.8 1.9 shard_map.181
  193.7 0.1 collective-permute-start.6
  193.8 4.6 %collective-permute-done.6 = f32[2,16,1024]{2,1,0:T(8,128)S(1)} collective-permute-done((f32[2,16,1024]{2,1,0:T(8,128)S(1)}, f32[2,16,1024]{2,1,0:T(8,128)S(1)}, u32[]{:S(2)}, u32[]{:S(2)}) %collective-permute-start.6) | collective-permute-done | bytes 131104 | tf_op jit(solution)/shard_map/ppermute | solution.py:429
  198.4 0.7 add_bitcast_fusion
  (30 shorter events, 0.2 us)
Async XLA Ops:
  0.0 0.7 copy-start.18
  0.7 0.9 copy-start.2
  1.6 0.8 copy-start.7
  2.5 1.2 copy-start.11
  3.7 0.9 copy-start.14
  4.6 0.9 copy-start.15
  5.5 0.9 copy-start.16
  6.4 0.9 copy-start.17
  7.3 0.7 copy-start.19
  11.2 26.6 %copy-start.13 = (f32[2,8,128]{2,1,0:T(8,128)S(1)}, f32[2,8,128]{2,1,0:T(8,128)}, u32[]{:S(2)}) copy-start(f32[2,8,128]{2,1,0:T(8,128)} %constant.37.clone.refs_9_.refs_6_.refs_10_.refs_8_) | copy-start | bytes 24580
  11.2 26.6 %all-to-all-start = ((f32[64,1,1280]{2,1,0:T(1,128)}), f32[64,1,1280]{2,1,0:T(1,128)S(1)}, u32[]{:S(2)}, u32[]{:S(2)}) async-start(f32[64,1,1280]{2,1,0:T(1,128)} %copy.19), calls=%async_computation | async-start | bytes 655360 | tf_op jit(solution)/shard_map/all_to_all | solution.py:301
  24.5 13.3 %copy-start = (bf16[2,256,256]{2,1,0:T(8,128)(2,1)S(1)}, bf16[2,256,256]{2,1,0:T(8,128)(2,1)}, u32[]{:S(2)}) copy-start(bf16[2,256,256]{2,1,0:T(8,128)(2,1)} %constant.36.clone.refs_8_.refs_5_.refs_9_.refs_7_) | copy-start | bytes 786436
  24.5 13.3 %copy-start.4 = (f32[2,64,256]{2,1,0:T(8,128)S(1)}, f32[2,64,256]{2,1,0:T(8,128)}, u32[]{:S(2)}) copy-start(f32[2,64,256]{2,1,0:T(8,128)} %constant.38.clone.refs_10_.refs_7_.refs_11_.refs_9_) | copy-start | bytes 393220
  24.5 13.3 %copy-start.5 = (f32[2,64,256]{2,1,0:T(8,128)S(1)}, f32[2,64,256]{2,1,0:T(8,128)}, u32[]{:S(2)}) copy-start(f32[2,64,256]{2,1,0:T(8,128)} %constant.35.clone.refs_7_.refs_4_.refs_8_.refs_6_) | copy-start | bytes 393220
  24.6 13.3 %copy-start.9 = (bf16[128,192]{1,0:T(8,128)(2,1)S(1)}, bf16[128,192]{1,0:T(8,128)(2,1)}, u32[]{:S(2)}) copy-start(bf16[128,192]{1,0:T(8,128)(2,1)} %constant.34.clone.refs_6_.refs_3_.refs_7_.refs_5_) | copy-start | bytes 147460
  24.6 13.3 %copy-start.10 = (bf16[128,192]{1,0:T(8,128)(2,1)S(1)}, bf16[128,192]{1,0:T(8,128)(2,1)}, u32[]{:S(2)}) copy-start(bf16[128,192]{1,0:T(8,128)(2,1)} %constant.33.clone.refs_5_.refs_2_.refs_6_.refs_4_) | copy-start | bytes 147460
  24.6 13.2 %collective-permute-start.2 = (f32[64,512]{1,0:T(8,128)S(1)}, f32[64,512]{1,0:T(8,128)S(1)}, u32[]{:S(2)}, u32[]{:S(2)}) collective-permute-start(f32[64,512]{1,0:T(8,128)S(1)} %get-tuple-element.22.refs_1_.refs_2_), channel_id=1, source_target_pairs={{0,192},{128,64},{1,193},{129,65},{2,194},{130,66},{3,195},{131,67... | collective-permute-start | bytes 393224 | tf_op jit(solution)/shard_map/ppermute | solution.py:307
  29.1 8.7 %collective-permute-start.1 = (f32[64,512]{1,0:T(8,128)S(1)}, f32[64,512]{1,0:T(8,128)S(1)}, u32[]{:S(2)}, u32[]{:S(2)}) collective-permute-start(f32[64,512]{1,0:T(8,128)S(1)} %get-tuple-element.22.refs_1_.refs_2_), channel_id=1, source_target_pairs={{0,128},{128,0},{1,129},{129,1},{2,130},{130,2},{3,131},{131,3},{4... | collective-permute-start | bytes 393224 | tf_op jit(solution)/shard_map/ppermute | solution.py:307
  31.5 6.3 %collective-permute-start = (f32[64,512]{1,0:T(8,128)S(1)}, f32[64,512]{1,0:T(8,128)S(1)}, u32[]{:S(2)}, u32[]{:S(2)}) collective-permute-start(f32[64,512]{1,0:T(8,128)S(1)} %get-tuple-element.22.refs_1_.refs_2_), channel_id=1, source_target_pairs={{0,64},{128,192},{1,65},{129,193},{2,66},{130,194},{3,67},{131,195... | collective-permute-start | bytes 393224 | tf_op jit(solution)/shard_map/ppermute | solution.py:307
  39.2 24.6 %copy-start.8 = (bf16[128,192]{1,0:T(8,128)(2,1)S(1)}, bf16[128,192]{1,0:T(8,128)(2,1)}, u32[]{:S(2)}) copy-start(bf16[128,192]{1,0:T(8,128)(2,1)} %constant.28.clone.refs_4_.refs_5_.refs_6_) | copy-start | bytes 147460
  39.2 24.6 %copy-start.12 = (f32[2,8,256]{2,1,0:T(8,128)S(1)}, f32[2,8,256]{2,1,0:T(8,128)}, u32[]{:S(2)}) copy-start(f32[2,8,256]{2,1,0:T(8,128)} %constant.40.clone.refs_8_.refs_9_) | copy-start | bytes 49156
  40.0 23.8 %copy-start.1 = (bf16[2,256,256]{2,1,0:T(8,128)(2,1)S(1)}, bf16[2,256,256]{2,1,0:T(8,128)(2,1)}, u32[]{:S(2)}) copy-start(bf16[2,256,256]{2,1,0:T(8,128)(2,1)} %constant.39.clone.refs_7_.refs_8_) | copy-start | bytes 786436
  40.0 22.2 %all-to-all-start.1 = ((f32[64,1,512]{2,1,0:T(1,128)}), f32[64,1,512]{2,1,0:T(1,128)S(1)}, u32[]{:S(2)}, u32[]{:S(2)}) async-start(f32[64,1,512]{2,1,0:T(1,128)} %copy.20), calls=%async_computation.1 | async-start | bytes 262144 | tf_op jit(solution)/shard_map/all_to_all | solution.py:301
  51.8 12.0 %copy-start.3 = (f32[2,64,256]{2,1,0:T(8,128)S(1)}, f32[2,64,256]{2,1,0:T(8,128)}, u32[]{:S(2)}) copy-start(f32[2,64,256]{2,1,0:T(8,128)} %constant.29.clone.refs_5_.refs_6_.refs_7_) | copy-start | bytes 393220
  51.8 12.0 %copy-start.6 = (f32[2,64,256]{2,1,0:T(8,128)S(1)}, f32[2,64,256]{2,1,0:T(8,128)}, u32[]{:S(2)}) copy-start(f32[2,64,256]{2,1,0:T(8,128)} %constant.41.clone.refs_9_.refs_10_) | copy-start | bytes 393220
  51.8 10.4 %collective-permute-start.5 = (f32[64,512]{1,0:T(8,128)S(1)}, f32[64,512]{1,0:T(8,128)S(1)}, u32[]{:S(2)}, u32[]{:S(2)}) collective-permute-start(f32[64,512]{1,0:T(8,128)S(1)} %get-tuple-element.24.refs_1_.refs_2_), channel_id=1, source_target_pairs={{64,0},{192,128},{65,1},{193,129},{66,2},{194,130},{67,3},{195,131... | collective-permute-start | bytes 393224 | tf_op jit(solution)/shard_map/ppermute | solution.py:307
  53.2 8.9 %collective-permute-start.4 = (f32[64,512]{1,0:T(8,128)S(1)}, f32[64,512]{1,0:T(8,128)S(1)}, u32[]{:S(2)}, u32[]{:S(2)}) collective-permute-start(f32[64,512]{1,0:T(8,128)S(1)} %get-tuple-element.24.refs_1_.refs_2_), channel_id=1, source_target_pairs={{64,192},{192,64},{65,193},{193,65},{66,194},{194,66},{67,195},{19... | collective-permute-start | bytes 393224 | tf_op jit(solution)/shard_map/ppermute | solution.py:307
  53.9 9.8 %collective-permute-start.3 = (f32[64,512]{1,0:T(8,128)S(1)}, f32[64,512]{1,0:T(8,128)S(1)}, u32[]{:S(2)}, u32[]{:S(2)}) collective-permute-start(f32[64,512]{1,0:T(8,128)S(1)} %get-tuple-element.24.refs_1_.refs_2_), channel_id=1, source_target_pairs={{64,128},{192,0},{65,129},{193,1},{66,130},{194,2},{67,131},{195,3... | collective-permute-start | bytes 393224 | tf_op jit(solution)/shard_map/ppermute | solution.py:307
  193.7 4.7 %collective-permute-start.6 = (f32[2,16,1024]{2,1,0:T(8,128)S(1)}, f32[2,16,1024]{2,1,0:T(8,128)S(1)}, u32[]{:S(2)}, u32[]{:S(2)}) collective-permute-start(f32[2,16,1024]{2,1,0:T(8,128)S(1)} %get-tuple-element.36), channel_id=1, source_target_pairs={{0,64},{64,0},{128,192},{192,128},{1,65},{65,1},{129,193},{193,129... | collective-permute-start | bytes 393224 | tf_op jit(solution)/shard_map/ppermute | solution.py:429

commit v2 on v1

--- a/solution.py
+++ b/solution.py
@@ -93,7 +93,22 @@
     return tab
 
 
-TAB = make_tables()
+def packed(tab):
+    wide = lambda table: np.pad(np.asarray(table), ((0, 0), (0, L - table.shape[1])))
+    rows = lambda parts: np.concatenate([wide(part) for part in parts], axis=0)
+    both = lambda names: np.stack([rows([tab[n][part] for n in names]) for part in range(2)])
+    return {
+        "y16": rows([tab["ly"], tab["ry"][0], tab["ry"][1]]),
+        "y32": both(("ty", "hy", "by")),
+        "x16": rows([tab["lxf"], tab["lxi"], tab["rx"][0], tab["rx"][1], tab["pm"]]),
+        "x32": both(("tx", "hx", "bx")),
+        "first32": both(("ty", "by0")),
+        "ry0": tab["ry0"],
+        "ly": tab["ly"],
+    }
+
+
+TAB = packed(make_tables())
 
 
 def mul(a, t):
@@ -207,15 +222,40 @@
     return jnp.concatenate(parts, axis=0).T
 
 
-Y_TABLES = ("ly", "ty", "ry", "by", "hy")
-X_TABLES = ("lxf", "lxi", "tx", "rx", "bx", "hx")
+def unpacked(axis, small, large):
+    tab = {}
+    if axis == "y":
+        tab["ly"] = small[0:128, 0:192]
+        tab["ry"] = (small[128:384, :], small[384:640, :])
+    else:
+        tab["lxf"], tab["lxi"] = small[0:128, 0:192], small[128:256, 0:192]
+        tab["rx"] = (small[256:512, :], small[512:768, :])
+        tab["pm"] = small[768:1024, :]
+    for name, at, lanes in (("t", slice(0, 64), L), ("h", slice(64, 128), L)):
+        tab[name + axis] = tuple(large[part, at, 0:lanes] for part in range(2))
+    lanes = L if axis == "y" else 128
+    tab["b" + axis] = tuple(large[part, 128:136, 0:lanes] for part in range(2))
+    return tab
 
 
 def parts_of(value, at=0):
     return value[:, at : at + L], value[:, at + L : at + 2 * L]
 
 
-def first_math(tab, obj, probe, target, dy, dx, row_pos):
+def split3(value):
+    high = value.astype(bf16)
+    rest = value - high.astype(f32)
+    middle = rest.astype(bf16)
+    return jnp.concatenate([high, middle, (rest - middle.astype(f32)).astype(bf16)], axis=0)
+
+
+def lanes_permuted(value, table):
+    rows = value.shape[0]
+    moved = jnp.dot(split3(value), table, preferred_element_type=f32)
+    return moved[:rows] + (moved[rows : 2 * rows] + moved[2 * rows :])
+
+
+def ramp_of(dy, dx, row_pos):
     lanes = lax.broadcasted_iota(jnp.int32, (8, N), 1)
     which = lax.broadcasted_iota(jnp.int32, (8, N), 0)
     turns = (lanes * dy - 256 * which) & (N - 1)
@@ -226,23 +266,15 @@
     turns = (kx * dx - 256 * lane) & (N - 1)
     wave = jnp.cos(turns.astype(f32) * f32(2.0 * math.pi / N))
     cos_x, sin_x = wave[:, 0:1], wave[:, 1:2]
-    ramp = (cos_y * cos_x - sin_y * sin_x, cos_y * sin_x + sin_y * cos_x)
-    shifted = mul_conj(probe, ramp)
-    spec = tuple(spread(x) for x in shifted)
+    return cos_y * cos_x - sin_y * sin_x, cos_y * sin_x + sin_y * cos_x
+
+
+def first_math(tab, probe, target, ramp):
+    spec = tuple(spread(x) for x in mul_conj(probe, ramp))
     spec = rows_join(*y_unfold(spec, tab["by0"]))
     out = times(jnp.concatenate(spec, axis=1), tab["ry0"])
     field = left(tab["ly"], mul((out[:, :L], out[:, L:]), tab["ty"]), -1)
-    target = spread(target)
-    high, rest = split2(target)
-    left_over = target - high.astype(f32)
-    middle = left_over.astype(bf16)
-    lowest = (left_over - middle.astype(f32)).astype(bf16)
-    moved = jnp.dot(
-        jnp.concatenate([high, middle, lowest], axis=0), tab["pm"], preferred_element_type=f32
-    )
-    target = moved[:B] + (moved[B : 2 * B] + moved[2 * B :])
-    planes = tuple(spread(x) for x in obj)
-    return jnp.concatenate(field + (target,) + planes, axis=1), jnp.concatenate(planes, axis=1)
+    return jnp.concatenate(field + (spread(target),), axis=1)
 
 
 def forward_of(axis):
@@ -259,42 +291,57 @@
     return inverse_of(axis)(times_h(spec, tab["h" + axis]), tab)
 
 
-def pick(own, others, pos, home):
-    out = own
-    for step, value in enumerate(others, start=1):
-        out = jnp.where((pos - home) % 4 == step, value, out)
-    return out
-
-
-VMEM_LIMIT = 40 * 1024 * 1024
-
-
-def call(body, names, operands, out_shapes, scalars=()):
-    tables = [jnp.asarray(TAB[name]) for name in names]
-    smem = len(scalars)
-    count = smem + len(operands)
+FIRST_LIMIT = 61 * 1024 * 1024
+VMEM_LIMIT = 16 * 1024 * 1024
+
+
+def call(body, axis, operands, out_shapes):
+    tables = [jnp.asarray(TAB[axis + bits]) for bits in ("16", "32")] if axis else []
+    count = len(operands)
 
     def kernel(*refs):
-        scalar_refs = refs[:smem]
-        ins = refs[smem:count]
-        table_refs = refs[count : count + len(names)]
-        outs = refs[count + len(names) :]
-        tab = {}
-        for name, ref in zip(names, table_refs):
-            if name in ("ly", "lxf", "lxi", "pm"):
-                tab[name] = ref[...]
-            else:
-                tab[name] = (ref[0], ref[1])
-        body(tab, scalar_refs, ins, outs)
+        tab = unpacked(axis, *refs[count : count + 2]) if axis else {}
+        body(tab, refs[:count], refs[count + len(tables) :])
 
     return pl.pallas_call(
         kernel,
         out_shape=[jax.ShapeDtypeStruct(shape, f32) for shape in out_shapes],
-        in_specs=[pl.BlockSpec(memory_space=pltpu.SMEM)] * smem
-        + [pl.BlockSpec(memory_space=pltpu.VMEM)] * (len(operands) + len(names)),
+        in_specs=[pl.BlockSpec(memory_space=pltpu.VMEM)] * (count + len(tables)),
         out_specs=[pl.BlockSpec(memory_space=pltpu.VMEM)] * len(out_shapes),
         compiler_params=pltpu.CompilerParams(vmem_limit_bytes=VMEM_LIMIT),
-    )(*scalars, *operands, *tables)
+    )(*operands, *tables)
+
+
+def first_call(probe, target, offsets):
+    names = ("ly", "first32", "ry0")
+
+    def kernel(offsets_ref, probe_ref, target_ref, ly, small, ry0, out):
+        wave = lax.axis_index("section") % 2
+        tab = {"ly": ly[...], "ry0": (ry0[0], ry0[1])}
+        tab["ty"] = (small[0, 0:64], small[1, 0:64])
+        tab["by0"] = (small[0, 64:72], small[1, 64:72])
+        ramp = ramp_of(offsets_ref[wave, 0], offsets_ref[wave, 1], lax.axis_index("row"))
+        out[...] = first_math(
+            tab,
+            (probe_ref[0], probe_ref[1]),
+            jnp.where(wave == 0, target_ref[0], target_ref[1]),
+            ramp,
+        )
+
+    arrays = [probe, target] + [jnp.asarray(TAB[name]) for name in names]
+
+    def whole(shape):
+        return pl.BlockSpec(shape, lambda i: (0,) * len(shape))
+
+    return pl.pallas_call(
+        kernel,
+        grid=(1,),
+        out_shape=jax.ShapeDtypeStruct((B, 3 * L), f32),
+        in_specs=[pl.BlockSpec((2, 2), lambda i: (0, 0), memory_space=pltpu.SMEM)]
+        + [whole(a.shape) for a in arrays],
+        out_specs=whole((B, 3 * L)),
+        compiler_params=pltpu.CompilerParams(vmem_limit_bytes=FIRST_LIMIT),
+    )(offsets, *arrays)
 
 
 def exchange(value):
@@ -302,130 +349,119 @@
 
 
 def shards(object_slices, probe_spec, offsets, measured):
-    def spread_slices(value, homes):
-        return [
-            lax.ppermute(value, "section", [(home, (home + step) % 4) for home in homes])
-            for step in (1, 2, 3)
-        ]
-
-    def first(tab, scalars, ins, outs):
-        wave = lax.axis_index("section") % 2
-        row_pos = lax.axis_index("row")
-        obj, probe, target = ins
-        sent, planes = first_math(
-            tab,
-            (obj[0, 0], obj[0, 1]),
-            (probe[0], probe[1]),
-            jnp.where(wave == 0, target[0], target[1]),
-            scalars[0][wave, 0],
-            scalars[0][wave, 1],
-            row_pos,
-        )
-        outs[0][...] = sent
-        outs[1][...] = planes
-
-    sent, planes = call(
-        first,
-        ("ly", "ty", "by0", "ry0", "pm"),
-        (object_slices, probe_spec, measured),
-        ((B, 5 * L), (B, 2 * L)),
-        scalars=(offsets,),
-    )
-    row_objects = spread_slices(planes, (0, 2))
-    got = exchange(sent)
-
-    def chosen(ins, home):
-        pos = lax.axis_index("section")
-        return parts_of(pick(ins[0], ins[1:], pos, home))
-
-    def second(tab, scalars, ins, outs):
+    own = object_slices[0]
+    raw = [lax.ppermute(own, "section", [(s, (s + k) % 4) for s in range(4)]) for k in (1, 2, 3)]
+    sent, *raw = lax.optimization_barrier((first_call(probe_spec, measured, offsets), *raw))
+    got1 = exchange(sent)
+
+    def arrange(tab, ins, outs):
+        place = lax.axis_index("section")
+        for layer in range(4):
+            turn = (place - layer) % 4
+            for part in range(2):
+                value = ins[0][part]
+                for k in (1, 2, 3):
+                    value = jnp.where(turn == k, ins[k][part], value)
+                outs[layer][:, part * L : part * L + L] = spread(value)
+
+    obj = call(arrange, "", (own, *raw), ((B, 2 * L),) * 4)
+
+    def second(tab, ins, outs):
         value = ins[0][...]
         psi = x_inverse(parts_of(value), tab)
         outs[0][...] = jnp.concatenate(psi, axis=1)
-        obj = chosen([ref[...] for ref in ins[1:]], 0)
-        a = propagate("x", mul(psi, obj), tab, False)
+        a = propagate("x", mul(psi, parts_of(ins[1][...])), tab, False)
+        outs[1][...] = jnp.concatenate(a + (ins[2][...],), axis=1)
+        outs[2][...] = lanes_permuted(value[:, 2 * L :], tab["pm"])
+
+    psi0, sent, target = call(
+        second,
+        "x",
+        (got1, obj[0], obj[1]),
+        ((B, 2 * L), (B, 4 * L), (B, L)),
+    )
+
+    def third(tab, ins, outs):
+        value = ins[0][...]
+        psi = propagate("y", parts_of(value), tab, False)
+        outs[0][...] = jnp.concatenate(psi, axis=1)
+        a = propagate("y", mul(psi, parts_of(value, 2 * L)), tab, False)
         outs[1][...] = jnp.concatenate(a, axis=1)
-        outs[2][...] = value[:, 3 * L :]
-        outs[3][...] = value[:, 2 * L : 3 * L]
-
-    psi0, sent, columns, target = call(
-        second,
-        X_TABLES,
-        (got, planes, *row_objects),
-        ((B, 2 * L), (B, 2 * L), (B, 2 * L), (B, L)),
-    )
-    column_objects = spread_slices(columns, (1, 3))
-    row_all = (planes, *row_objects)
-    column_all = (columns, *column_objects)
-
-    def inner(axis, home, last):
-        def body(tab, scalars, ins, outs):
-            psi = propagate(axis, parts_of(ins[0][...]), tab, False)
-            outs[0][...] = jnp.concatenate(psi, axis=1)
-            a = mul(psi, chosen([ref[...] for ref in ins[1:]], home))
-            a = y_forward(a, tab) if last else propagate(axis, a, tab, False)
-            outs[1][...] = jnp.concatenate(a, axis=1)
-
-        return body
-
-    square = ((B, 2 * L), (B, 2 * L))
-    psi1, sent = call(inner("y", 1, False), Y_TABLES, (exchange(sent), *column_all), square)
-    psi2, sent = call(inner("x", 2, False), X_TABLES, (exchange(sent), *row_all), square)
-    psi3, sent = call(inner("y", 3, True), Y_TABLES, (exchange(sent), *column_all), square)
-
-    def far(tab, scalars, ins, outs):
+
+    got2 = exchange(sent)
+    psi1, sent = call(third, "y", (got2,), ((B, 2 * L),) * 2)
+
+    def fourth(tab, ins, outs):
+        psi = propagate("x", parts_of(ins[0][...]), tab, False)
+        outs[0][...] = jnp.concatenate(psi, axis=1)
+        a = propagate("x", mul(psi, parts_of(ins[1][...])), tab, False)
+        outs[1][...] = jnp.concatenate(a + (ins[2][...],), axis=1)
+
+    psi2, sent = call(
+        fourth, "x", (exchange(sent), obj[2], obj[3]), ((B, 2 * L), (B, 4 * L))
+    )
+
+    def fifth(tab, ins, outs):
+        value = ins[0][...]
+        psi = propagate("y", parts_of(value), tab, False)
+        outs[0][...] = jnp.concatenate(psi, axis=1)
+        a = y_forward(mul(psi, parts_of(value, 2 * L)), tab)
+        outs[1][...] = jnp.concatenate(a, axis=1)
+
+    got4 = exchange(sent)
+    psi3, sent = call(fifth, "y", (got4,), ((B, 2 * L),) * 2)
+
+    def far(tab, ins, outs):
         phi = x_forward(parts_of(ins[0][...]), tab)
         weight = 0.5 * (phi[0] * phi[0] + phi[1] * phi[1] - ins[1][...])
         a = x_inverse((phi[0] * weight, phi[1] * weight), tab)
         outs[0][...] = jnp.concatenate(a, axis=1)
 
-    (sent,) = call(far, X_TABLES, (exchange(sent), target), ((B, 2 * L),))
-
-    def back(axis, home, top, both):
-        def body(tab, scalars, ins, outs):
-            a = parts_of(ins[0][...])
-            adj = y_inverse(a, tab) if top else propagate(axis, a, tab, True)
-            grad = mul_conj(adj, parts_of(ins[1][...]))
-            a = mul_conj(adj, chosen([ref[...] for ref in ins[2:]], home))
-            a = propagate(axis, a, tab, True)
-            if both:
-                outs[0][...] = jnp.concatenate(a + grad, axis=1)
-            else:
-                outs[0][...] = jnp.concatenate(a, axis=1)
-                outs[1][...] = jnp.concatenate(grad, axis=1)
-
-        return body
-
-    wide = ((B, 4 * L),)
-    (sent,) = call(back("y", 3, True, True), Y_TABLES, (exchange(sent), psi3, *column_all), wide)
-    got3 = exchange(sent)
-    sent, grad2 = call(back("x", 2, False, False), X_TABLES, (got3, psi2, *row_all), square)
-    (sent,) = call(back("y", 1, False, True), Y_TABLES, (exchange(sent), psi1, *column_all), wide)
-    got1 = exchange(sent)
-
-    def final(tab, scalars, ins, outs):
+    (sent,) = call(far, "x", (exchange(sent), target), ((B, 2 * L),))
+
+    def back_third(tab, ins, outs):
+        adj = y_inverse(parts_of(ins[0][...]), tab)
+        grad = mul_conj(adj, parts_of(ins[1][...]))
+        a = propagate("y", mul_conj(adj, parts_of(ins[2][...], 2 * L)), tab, True)
+        outs[0][...] = jnp.concatenate(a, axis=1)
+        outs[1][...] = jnp.concatenate(grad, axis=1)
+
+    square = ((B, 2 * L),) * 2
+    sent, grad3 = call(back_third, "y", (exchange(sent), psi3, got4), square)
+
+    def back_second(tab, ins, outs):
         adj = propagate("x", parts_of(ins[0][...]), tab, True)
-        grad0 = mul_conj(adj, parts_of(ins[1][...]))
-        grads = (
-            grad0,
-            parts_of(ins[0][...], 2 * L),
-            parts_of(ins[2][...]),
-            parts_of(ins[3][...], 2 * L),
-        )
+        grad = mul_conj(adj, parts_of(ins[1][...]))
+        a = propagate("x", mul_conj(adj, parts_of(ins[2][...])), tab, True)
+        outs[0][...] = jnp.concatenate(a, axis=1)
+        outs[1][...] = jnp.concatenate(grad, axis=1)
+
+    sent, grad2 = call(back_second, "x", (exchange(sent), psi2, obj[2]), square)
+
+    def back_first(tab, ins, outs):
+        adj = propagate("y", parts_of(ins[0][...]), tab, True)
+        grad = mul_conj(adj, parts_of(ins[1][...]))
+        a = propagate("y", mul_conj(adj, parts_of(ins[2][...], 2 * L)), tab, True)
+        ride = jnp.where(lax.axis_index("section") < 2, jnp.concatenate(grad, axis=1), ins[3][...])
+        outs[0][...] = jnp.concatenate(a + (ride,), axis=1)
+
+    (sent,) = call(
+        back_first, "y", (exchange(sent), psi1, got2, grad3), ((B, 4 * L),)
+    )
+
+    def last(tab, ins, outs):
+        value = ins[0][...]
+        adj = propagate("x", parts_of(value), tab, True)
+        grad = mul_conj(adj, parts_of(ins[1][...]))
         pos = lax.axis_index("section")
-        for out, target_pos in ((outs[0], pos), (outs[1], pos + 1 - 2 * (pos % 2))):
-            for part in range(2):
-                value = grads[0][part]
-                for layer in (1, 2, 3):
-                    value = jnp.where(target_pos == layer, grads[layer][part], value)
-                out[part] = collect(value)
-
-    kept, given = call(
-        final,
-        X_TABLES,
-        (got1, psi0, grad2, got3),
-        ((2, T, N), (2, T, N)),
-    )
+        other = parts_of(ins[2][...])
+        upper = parts_of(value, 2 * L)
+        for part in range(2):
+            lower = jnp.where(pos < 2, grad[part], other[part])
+            outs[0][part] = collect(jnp.where(pos % 2 == 0, lower, upper[part]))
+            outs[1][part] = collect(jnp.where(pos % 2 == 0, upper[part], lower))
+
+    kept, given = call(last, "x", (exchange(sent), psi0, grad2), ((2, T, N),) * 2)
     taken = lax.ppermute(given, "section", [(0, 1), (1, 0), (2, 3), (3, 2)])
     return (kept + taken)[None]
 

time: 200 us -> 189 us (0.945)
  starting transfers between devices: 36.8 us -> 17 us
  blocking collectives: 116 us -> 128 us
  local copies, waits for them, and re-layouts: 11.3 us -> 4.45 us
  Pallas kernels: 15.5 us -> 18.8 us
    all_to_all x2 -> x1, starting transfers between devices: 25.1 us -> 12.5 us  [exchange(): return lax.all_to_all(value, 'row', split_axis=0, concat_axis=0, tiled=True)]
    all_to_all x7 -> x8, blocking collectives: 116 us -> 128 us  [exchange(): return lax.all_to_all(value, 'row', split_axis=0, concat_axis=0, tiled=True)]
    ppermute x6 -> x3, starting transfers between devices: 11.6 us -> 4.43 us  [shards(): lax.ppermute(own, 'section', [(s, (s + k) % 4) for s in range(4)])]
    unnamed x49 -> x19, local copies, waits for them, and re-layouts: 8.22 us -> 1.14 us
    ppermute x6 -> x3, waiting for transfers between devices: 1.57 us -> 5.2 us  [shards(): lax.ppermute(own, 'section', [(s, (s + k) % 4) for s in range(4)])]
    pallas_call x0 -> x1, Pallas kernels: none -> 3.42 us  [first_call(): pl.pallas_call(kernel, grid=(1,), out_shape=jax.ShapeDtypeStruct((B, 3 *...]
    all_to_all x2 -> x1, waiting for transfers between devices: 11.9 us -> 8.77 us  [exchange(): return lax.all_to_all(value, 'row', split_axis=0, concat_axis=0, tiled=True)]
  transfers between devices with their start and end apart: 9 -> 5, of which waited for: 4 -> 4; matrix products, arithmetic and copies ran while one was open for 0% -> 0% of each run, Pallas kernels for 0% -> 3%
where the time goes in v2:
time: 189 us; the launch traced here: 188 us
  blocking collectives  128 us (68%)
  Pallas kernels  18.8 us (10%)
  waiting for transfers between devices  18.6 us (10%)
  starting transfers between devices  17 us (9%)
  local copies, waits for them, and re-layouts  4.45 us (2%)
    all_to_all x8, blocking collectives, exchange(): return lax.all_to_all(value, 'row', split_axis=0, concat_axis=0, tiled=True)  128 us
    pallas_call x10, Pallas kernels, call(): pl.pallas_call(kernel, out_shape=[jax.ShapeDtypeStruct(shape, f32) for sh...  15.4 us
    all_to_all x1, starting transfers between devices, exchange(): return lax.all_to_all(value, 'row', split_axis=0, concat_axis=0, tiled=True)  12.5 us
    all_to_all x1, waiting for transfers between devices, exchange(): return lax.all_to_all(value, 'row', split_axis=0, concat_axis=0, tiled=True)  8.77 us
    ppermute x3, waiting for transfers between devices, shards(): lax.ppermute(own, 'section', [(s, (s + k) % 4) for s in range(4)])  5.2 us
    ppermute x1, waiting for transfers between devices, shards(): taken = lax.ppermute(given, 'section', [(0, 1), (1, 0), (2, 3), (3, 2)])  4.61 us
    ppermute x3, starting transfers between devices, shards(): lax.ppermute(own, 'section', [(s, (s + k) % 4) for s in range(4)])  4.43 us
  transfers between devices with their start and end apart: 5, of which 4 were waited for; matrix products, arithmetic and copies ran while one was open for 0% of the time, Pallas kernels for 3%

profile of v2, /device:TPU:1, one launch (start us, length us, event | category | flops | bytes accessed | tf_op | source)
XLA Modules:
  0.0 188.2 jit_solution(7875857554297229360)
XLA Ops:
  0.0 3.3 %collective-permute-start.2 = (f32[2,16,1024]{2,1,0:T(8,128)}, f32[2,16,1024]{2,1,0:T(8,128)S(1)}, u32[]{:S(2)}, u32[]{:S(2)}) collective-permute-start(f32[2,16,1024]{2,1,0:T(8,128)} %bitcast.58), channel_id=1, source_target_pairs={{0,192},{64,0},{128,64},{192,128},{1,193},{65,1},{129,65},{193,129... | collective-permute-start | bytes 393224 | tf_op jit(solution)/shard_map/ppermute | solution.py:353
  3.3 0.5 collective-permute-start.1
  3.8 0.6 collective-permute-start
  4.4 3.4 %shard_map.109 = f32[64,768]{1,0:T(8,128)} custom-call(s32[2,2]{1,0:T(2,128)} %offsets_ref.1, f32[2,16,1024]{2,1,0:T(8,128)} %probe_ref.1, f32[2,16,1024]{2,1,0:T(8,128)} %target_ref.1, bf16[128,192]{1,0:T(8,128)(2,1)} %constant.14.clone.ly, f32[2,72,256]{2,1,0:T(8,128)} %constant.15.clone.small, bf16[2,512,512]{2,1,0:T(8,128)(2,1)} %constant.16.clone.ry0), custom_call_target="tpu_custom_call" | custom-call | tf_op jit(solution)/shard_map/pallas_call | solution.py:336
  7.9 0.0 collective-permute-done.2.refs_3_
  7.9 1.1 collective-permute-done.1.refs_2_
  8.9 4.1 %collective-permute-done.refs_1_ = f32[2,16,1024]{2,1,0:T(8,128)S(1)} collective-permute-done((f32[2,16,1024]{2,1,0:T(8,128)}, f32[2,16,1024]{2,1,0:T(8,128)S(1)}, u32[]{:S(2)}, u32[]{:S(2)}) %collective-permute-start) | collective-permute-done | bytes 131104 | tf_op jit(solution)/shard_map/ppermute | solution.py:353
  13.1 1.8 copy.12
  14.9 0.0 copy-start.4
  14.9 12.5 %all-to-all-start = ((f32[64,1,768]{2,1,0:T(1,128)}), f32[64,1,768]{2,1,0:T(1,128)S(1)}, u32[]{:S(2)}, u32[]{:S(2)}) async-start(f32[64,1,768]{2,1,0:T(1,128)} %copy.12), calls=%async_computation | async-start | bytes 393216 | tf_op jit(solution)/shard_map/all_to_all | solution.py:348
  27.4 0.0 copy-done.4
  27.4 0.0 copy-start
  27.4 2.1 %shard_map.110 = (f32[64,512]{1,0:T(8,128)S(1)}, f32[64,512]{1,0:T(8,128)S(1)}, f32[64,512]{1,0:T(8,128)S(1)}, f32[64,512]{1,0:T(8,128)S(1)}) custom-call(f32[2,16,1024]{2,1,0:T(8,128)S(1)} %bitcast.61, f32[2,16,1024]{2,1,0:T(8,128)S(1)} %collective-permute-done.refs_1_, f32[2,16,1024]{2,1,0:T(8,128)S(1)} %collective-permute-done.1.refs_2_, ...), custom_call_target="tpu_custom_call" | custom-call | tf_op jit(solution)/shard_map/pallas_call | solution.py:306
  29.5 0.0 copy-start.1
  29.5 8.8 %all-to-all-done = f32[64,1,768]{2,1,0:T(1,128)S(1)} async-done(((f32[64,1,768]{2,1,0:T(1,128)}), f32[64,1,768]{2,1,0:T(1,128)S(1)}, u32[]{:S(2)}, u32[]{:S(2)}) %all-to-all-start) | async-done | bytes 196640 | tf_op jit(solution)/shard_map/all_to_all | solution.py:348
  38.3 0.0 copy-done
  38.3 0.0 copy-done.1
  38.3 1.3 shard_map.111
  39.6 0.3 copy.13
  39.9 0.0 copy-start.3
  39.9 17.6 %all_to_all.99 = f32[64,1,1024]{2,1,0:T(1,128)S(1)} all-to-all(f32[64,1,1024]{2,1,0:T(1,128)S(1)} %copy.13), channel_id=1, replica_groups=mesh['section'=4,'row'=64] {'row'}, dimensions={0} | all-to-all | bytes 524288 | tf_op jit(solution)/shard_map/all_to_all | solution.py:348
  57.5 0.0 copy-start.2
  57.6 0.0 copy-done.3
  57.6 0.9 copy-done.2
  58.5 1.7 shard_map.112
  60.2 0.1 copy.14
  60.3 16.2 %all_to_all.100 = f32[64,1,512]{2,1,0:T(1,128)S(1)} all-to-all(f32[64,1,512]{2,1,0:T(1,128)S(1)} %copy.14), channel_id=1, replica_groups=mesh['section'=4,'row'=64] {'row'}, dimensions={0} | all-to-all | bytes 262144 | tf_op jit(solution)/shard_map/all_to_all | solution.py:348
  76.5 1.7 shard_map.113
  78.2 0.3 copy.15
  78.5 16.7 %all_to_all.101 = f32[64,1,1024]{2,1,0:T(1,128)S(1)} all-to-all(f32[64,1,1024]{2,1,0:T(1,128)S(1)} %copy.15), channel_id=1, replica_groups=mesh['section'=4,'row'=64] {'row'}, dimensions={0} | all-to-all | bytes 524288 | tf_op jit(solution)/shard_map/all_to_all | solution.py:348
  95.2 1.2 shard_map.114
  96.5 0.1 copy.16
  96.6 16.2 %all_to_all.102 = f32[64,1,512]{2,1,0:T(1,128)S(1)} all-to-all(f32[64,1,512]{2,1,0:T(1,128)S(1)} %copy.16), channel_id=1, replica_groups=mesh['section'=4,'row'=64] {'row'}, dimensions={0} | all-to-all | bytes 262144 | tf_op jit(solution)/shard_map/all_to_all | solution.py:348
  112.8 0.9 shard_map.115
  113.7 0.1 copy.17
  113.8 15.0 %all_to_all.103 = f32[64,1,512]{2,1,0:T(1,128)S(1)} all-to-all(f32[64,1,512]{2,1,0:T(1,128)S(1)} %copy.17), channel_id=1, replica_groups=mesh['section'=4,'row'=64] {'row'}, dimensions={0} | all-to-all | bytes 262144 | tf_op jit(solution)/shard_map/all_to_all | solution.py:348
  128.9 1.3 shard_map.116
  130.1 0.1 copy.18
  130.3 15.0 %all_to_all.104 = f32[64,1,512]{2,1,0:T(1,128)S(1)} all-to-all(f32[64,1,512]{2,1,0:T(1,128)S(1)} %copy.18), channel_id=1, replica_groups=mesh['section'=4,'row'=64] {'row'}, dimensions={0} | all-to-all | bytes 262144 | tf_op jit(solution)/shard_map/all_to_all | solution.py:348
  145.3 1.7 shard_map.117
  147.1 0.1 copy.19
  147.2 15.0 %all_to_all.105 = f32[64,1,512]{2,1,0:T(1,128)S(1)} all-to-all(f32[64,1,512]{2,1,0:T(1,128)S(1)} %copy.19), channel_id=1, replica_groups=mesh['section'=4,'row'=64] {'row'}, dimensions={0} | all-to-all | bytes 262144 | tf_op jit(solution)/shard_map/all_to_all | solution.py:348
  162.3 1.7 shard_map.118
  163.9 0.3 copy.20
  164.2 16.7 %all_to_all.106 = f32[64,1,1024]{2,1,0:T(1,128)S(1)} all-to-all(f32[64,1,1024]{2,1,0:T(1,128)S(1)} %copy.20), channel_id=1, replica_groups=mesh['section'=4,'row'=64] {'row'}, dimensions={0} | all-to-all | bytes 524288 | tf_op jit(solution)/shard_map/all_to_all | solution.py:348
  180.9 1.9 %shard_map.119 = (f32[2,16,1024]{2,1,0:T(8,128)S(1)}, f32[2,16,1024]{2,1,0:T(8,128)S(1)}) custom-call(f32[64,1024]{1,0:T(8,128)S(1)} %bitcast.43, f32[64,512]{1,0:T(8,128)S(1)} %get-tuple-element.47.refs_1_, f32[64,512]{1,0:T(8,128)S(1)} %get-tuple-element.48.refs_2_, bf16[1024,256]{1,0:T(8,128)(2,1)S(1)} %copy-done, f32[2,136,256]{2,1,0:T(8,128)S(1)} %copy-done.1), custom_call_target="tpu_custom_call" | custom-call | tf_op jit(solution)/shard_map/pallas_call | solution.py:306
  182.9 0.1 collective-permute-start.3
  182.9 4.6 %collective-permute-done.3 = f32[2,16,1024]{2,1,0:T(8,128)S(1)} collective-permute-done((f32[2,16,1024]{2,1,0:T(8,128)S(1)}, f32[2,16,1024]{2,1,0:T(8,128)S(1)}, u32[]{:S(2)}, u32[]{:S(2)}) %collective-permute-start.3) | collective-permute-done | bytes 131104 | tf_op jit(solution)/shard_map/ppermute | solution.py:465
  187.5 0.7 add_bitcast_fusion
  (9 shorter events, 0.2 us)
Async XLA Ops:
  0.0 7.9 %collective-permute-start.2 = (f32[2,16,1024]{2,1,0:T(8,128)}, f32[2,16,1024]{2,1,0:T(8,128)S(1)}, u32[]{:S(2)}, u32[]{:S(2)}) collective-permute-start(f32[2,16,1024]{2,1,0:T(8,128)} %bitcast.58), channel_id=1, source_target_pairs={{0,192},{64,0},{128,64},{192,128},{1,193},{65,1},{129,65},{193,129... | collective-permute-start | bytes 393224 | tf_op jit(solution)/shard_map/ppermute | solution.py:353
  3.3 5.6 %collective-permute-start.1 = (f32[2,16,1024]{2,1,0:T(8,128)}, f32[2,16,1024]{2,1,0:T(8,128)S(1)}, u32[]{:S(2)}, u32[]{:S(2)}) collective-permute-start(f32[2,16,1024]{2,1,0:T(8,128)} %bitcast.59), channel_id=1, source_target_pairs={{0,128},{64,192},{128,0},{192,64},{1,129},{65,193},{129,1},{193,65... | collective-permute-start | bytes 393224 | tf_op jit(solution)/shard_map/ppermute | solution.py:353
  3.8 9.2 %collective-permute-start = (f32[2,16,1024]{2,1,0:T(8,128)}, f32[2,16,1024]{2,1,0:T(8,128)S(1)}, u32[]{:S(2)}, u32[]{:S(2)}) collective-permute-start(f32[2,16,1024]{2,1,0:T(8,128)} %bitcast.60), channel_id=1, source_target_pairs={{0,64},{64,128},{128,192},{192,0},{1,65},{65,129},{129,193},{193,1... | collective-permute-start | bytes 393224 | tf_op jit(solution)/shard_map/ppermute | solution.py:353
  14.9 12.5 %copy-start.4 = (f32[1,2,16,1024]{3,2,1,0:T(8,128)S(1)}, f32[1,2,16,1024]{3,2,1,0:T(8,128)}, u32[]{:S(2)}) copy-start(f32[1,2,16,1024]{3,2,1,0:T(8,128)} %param.11) | copy-start | bytes 393220
  14.9 23.4 %all-to-all-start = ((f32[64,1,768]{2,1,0:T(1,128)}), f32[64,1,768]{2,1,0:T(1,128)S(1)}, u32[]{:S(2)}, u32[]{:S(2)}) async-start(f32[64,1,768]{2,1,0:T(1,128)} %copy.12), calls=%async_computation | async-start | bytes 393216 | tf_op jit(solution)/shard_map/all_to_all | solution.py:348
  27.4 10.9 %copy-start = (bf16[1024,256]{1,0:T(8,128)(2,1)S(1)}, bf16[1024,256]{1,0:T(8,128)(2,1)}, u32[]{:S(2)}) copy-start(bf16[1024,256]{1,0:T(8,128)(2,1)} %constant.17.clone.refs_3_.refs_2_) | copy-start | bytes 1572868
  29.5 8.8 %copy-start.1 = (f32[2,136,256]{2,1,0:T(8,128)S(1)}, f32[2,136,256]{2,1,0:T(8,128)}, u32[]{:S(2)}) copy-start(f32[2,136,256]{2,1,0:T(8,128)} %constant.18.clone.refs_4_.refs_3_) | copy-start | bytes 835588
  39.9 17.7 %copy-start.3 = (f32[2,136,256]{2,1,0:T(8,128)S(1)}, f32[2,136,256]{2,1,0:T(8,128)}, u32[]{:S(2)}) copy-start(f32[2,136,256]{2,1,0:T(8,128)} %constant.20.clone.refs_2_.refs_4_.refs_5_) | copy-start | bytes 835588
  57.5 1.0 copy-start.2
  182.9 4.7 %collective-permute-start.3 = (f32[2,16,1024]{2,1,0:T(8,128)S(1)}, f32[2,16,1024]{2,1,0:T(8,128)S(1)}, u32[]{:S(2)}, u32[]{:S(2)}) collective-permute-start(f32[2,16,1024]{2,1,0:T(8,128)S(1)} %get-tuple-element.50), channel_id=1, source_target_pairs={{0,64},{64,0},{128,192},{192,128},{1,65},{65,1},{129,193},{193,129... | collective-permute-start | bytes 393224 | tf_op jit(solution)/shard_map/ppermute | solution.py:465

commit v3 on v2

--- a/solution.py
+++ b/solution.py
@@ -111,6 +111,19 @@
 TAB = packed(make_tables())
 
 
+def wide(ref):
+    count = ref.shape[0] // B
+    return jnp.concatenate(
+        [ref[pl.ds(i, B, stride=count), :] for i in range(count)], axis=1
+    )
+
+
+def put(ref, value):
+    count = ref.shape[0] // B
+    for i in range(count):
+        ref[pl.ds(i, B, stride=count), :] = value[:, 128 * i : 128 * i + 128]
+
+
 def mul(a, t):
     return a[0] * t[0] - a[1] * t[1], a[0] * t[1] + a[1] * t[0]
 
@@ -274,7 +287,7 @@
     spec = rows_join(*y_unfold(spec, tab["by0"]))
     out = times(jnp.concatenate(spec, axis=1), tab["ry0"])
     field = left(tab["ly"], mul((out[:, :L], out[:, L:]), tab["ty"]), -1)
-    return jnp.concatenate(field + (spread(target),), axis=1)
+    return jnp.concatenate(field + (spread(target), jnp.zeros((B, L), f32)), axis=1)
 
 
 def forward_of(axis):
@@ -321,12 +334,13 @@
         tab["ty"] = (small[0, 0:64], small[1, 0:64])
         tab["by0"] = (small[0, 64:72], small[1, 64:72])
         ramp = ramp_of(offsets_ref[wave, 0], offsets_ref[wave, 1], lax.axis_index("row"))
-        out[...] = first_math(
+        value = first_math(
             tab,
             (probe_ref[0], probe_ref[1]),
             jnp.where(wave == 0, target_ref[0], target_ref[1]),
             ramp,
         )
+        put(out, value)
 
     arrays = [probe, target] + [jnp.asarray(TAB[name]) for name in names]
 
@@ -336,10 +350,10 @@
     return pl.pallas_call(
         kernel,
         grid=(1,),
-        out_shape=jax.ShapeDtypeStruct((B, 3 * L), f32),
+        out_shape=jax.ShapeDtypeStruct((8 * B, 128), f32),
         in_specs=[pl.BlockSpec((2, 2), lambda i: (0, 0), memory_space=pltpu.SMEM)]
         + [whole(a.shape) for a in arrays],
-        out_specs=whole((B, 3 * L)),
+        out_specs=whole((8 * B, 128)),
         compiler_params=pltpu.CompilerParams(vmem_limit_bytes=FIRST_LIMIT),
     )(offsets, *arrays)
 
@@ -367,90 +381,90 @@
     obj = call(arrange, "", (own, *raw), ((B, 2 * L),) * 4)
 
     def second(tab, ins, outs):
-        value = ins[0][...]
+        value = wide(ins[0])
         psi = x_inverse(parts_of(value), tab)
         outs[0][...] = jnp.concatenate(psi, axis=1)
         a = propagate("x", mul(psi, parts_of(ins[1][...])), tab, False)
-        outs[1][...] = jnp.concatenate(a + (ins[2][...],), axis=1)
-        outs[2][...] = lanes_permuted(value[:, 2 * L :], tab["pm"])
+        put(outs[1], jnp.concatenate(a + (ins[2][...],), axis=1))
+        outs[2][...] = lanes_permuted(value[:, 2 * L : 3 * L], tab["pm"])
 
     psi0, sent, target = call(
         second,
         "x",
         (got1, obj[0], obj[1]),
-        ((B, 2 * L), (B, 4 * L), (B, L)),
+        ((B, 2 * L), (8 * B, 128), (B, L)),
     )
 
     def third(tab, ins, outs):
-        value = ins[0][...]
+        value = wide(ins[0])
         psi = propagate("y", parts_of(value), tab, False)
         outs[0][...] = jnp.concatenate(psi, axis=1)
         a = propagate("y", mul(psi, parts_of(value, 2 * L)), tab, False)
-        outs[1][...] = jnp.concatenate(a, axis=1)
+        put(outs[1], jnp.concatenate(a, axis=1))
 
     got2 = exchange(sent)
-    psi1, sent = call(third, "y", (got2,), ((B, 2 * L),) * 2)
+    psi1, sent = call(third, "y", (got2,), ((B, 2 * L), (4 * B, 128)))
 
     def fourth(tab, ins, outs):
-        psi = propagate("x", parts_of(ins[0][...]), tab, False)
+        psi = propagate("x", parts_of(wide(ins[0])), tab, False)
         outs[0][...] = jnp.concatenate(psi, axis=1)
         a = propagate("x", mul(psi, parts_of(ins[1][...])), tab, False)
-        outs[1][...] = jnp.concatenate(a + (ins[2][...],), axis=1)
+        put(outs[1], jnp.concatenate(a + (ins[2][...],), axis=1))
 
     psi2, sent = call(
-        fourth, "x", (exchange(sent), obj[2], obj[3]), ((B, 2 * L), (B, 4 * L))
+        fourth, "x", (exchange(sent), obj[2], obj[3]), ((B, 2 * L), (8 * B, 128))
     )
 
     def fifth(tab, ins, outs):
-        value = ins[0][...]
+        value = wide(ins[0])
         psi = propagate("y", parts_of(value), tab, False)
         outs[0][...] = jnp.concatenate(psi, axis=1)
         a = y_forward(mul(psi, parts_of(value, 2 * L)), tab)
-        outs[1][...] = jnp.concatenate(a, axis=1)
+        put(outs[1], jnp.concatenate(a, axis=1))
 
     got4 = exchange(sent)
-    psi3, sent = call(fifth, "y", (got4,), ((B, 2 * L),) * 2)
+    psi3, sent = call(fifth, "y", (got4,), ((B, 2 * L), (4 * B, 128)))
 
     def far(tab, ins, outs):
-        phi = x_forward(parts_of(ins[0][...]), tab)
+        phi = x_forward(parts_of(wide(ins[0])), tab)
         weight = 0.5 * (phi[0] * phi[0] + phi[1] * phi[1] - ins[1][...])
         a = x_inverse((phi[0] * weight, phi[1] * weight), tab)
-        outs[0][...] = jnp.concatenate(a, axis=1)
-
-    (sent,) = call(far, "x", (exchange(sent), target), ((B, 2 * L),))
+        put(outs[0], jnp.concatenate(a, axis=1))
+
+    (sent,) = call(far, "x", (exchange(sent), target), ((4 * B, 128),))
 
     def back_third(tab, ins, outs):
-        adj = y_inverse(parts_of(ins[0][...]), tab)
+        adj = y_inverse(parts_of(wide(ins[0])), tab)
         grad = mul_conj(adj, parts_of(ins[1][...]))
-        a = propagate("y", mul_conj(adj, parts_of(ins[2][...], 2 * L)), tab, True)
-        outs[0][...] = jnp.concatenate(a, axis=1)
+        a = propagate("y", mul_conj(adj, parts_of(wide(ins[2]), 2 * L)), tab, True)
+        put(outs[0], jnp.concatenate(a, axis=1))
         outs[1][...] = jnp.concatenate(grad, axis=1)
 
-    square = ((B, 2 * L),) * 2
+    square = ((4 * B, 128), (B, 2 * L))
     sent, grad3 = call(back_third, "y", (exchange(sent), psi3, got4), square)
 
     def back_second(tab, ins, outs):
-        adj = propagate("x", parts_of(ins[0][...]), tab, True)
+        adj = propagate("x", parts_of(wide(ins[0])), tab, True)
         grad = mul_conj(adj, parts_of(ins[1][...]))
         a = propagate("x", mul_conj(adj, parts_of(ins[2][...])), tab, True)
-        outs[0][...] = jnp.concatenate(a, axis=1)
+        put(outs[0], jnp.concatenate(a, axis=1))
         outs[1][...] = jnp.concatenate(grad, axis=1)
 
     sent, grad2 = call(back_second, "x", (exchange(sent), psi2, obj[2]), square)
 
     def back_first(tab, ins, outs):
-        adj = propagate("y", parts_of(ins[0][...]), tab, True)
+        adj = propagate("y", parts_of(wide(ins[0])), tab, True)
         grad = mul_conj(adj, parts_of(ins[1][...]))
-        a = propagate("y", mul_conj(adj, parts_of(ins[2][...], 2 * L)), tab, True)
+        a = propagate("y", mul_conj(adj, parts_of(wide(ins[2]), 2 * L)), tab, True)
         ride = jnp.where(lax.axis_index("section") < 2, jnp.concatenate(grad, axis=1), ins[3][...])
-        outs[0][...] = jnp.concatenate(a + (ride,), axis=1)
+        put(outs[0], jnp.concatenate(a + (ride,), axis=1))
 
     (sent,) = call(
-        back_first, "y", (exchange(sent), psi1, got2, grad3), ((B, 4 * L),)
+        back_first, "y", (exchange(sent), psi1, got2, grad3), ((8 * B, 128),)
     )
 
     def last(tab, ins, outs):
-        value = ins[0][...]
+        value = wide(ins[0])
         adj = propagate("x", parts_of(value), tab, True)
         grad = mul_conj(adj, parts_of(ins[1][...]))
         pos = lax.axis_index("section")

time: 189 us -> 186 us (0.984)
  local copies, waits for them, and re-layouts: 4.45 us -> 0.02 us
    all_to_all x9 -> x0, local copies, waits for them, and re-layouts: 3.31 us -> none  [exchange(): return lax.all_to_all(value, 'row', split_axis=0, concat_axis=0, tiled=True)]
where the time goes in v3:
time: 186 us; the launch traced here: 185 us
  blocking collectives  129 us (69%)
  waiting for transfers between devices  19.6 us (11%)
  Pallas kernels  18.9 us (10%)
  starting transfers between devices  17 us (9%)
    all_to_all x8, blocking collectives, exchange(): return lax.all_to_all(value, 'row', split_axis=0, concat_axis=0, tiled=True)  129 us
    pallas_call x10, Pallas kernels, call(): pl.pallas_call(kernel, out_shape=[jax.ShapeDtypeStruct(shape, f32) for sh...  15.4 us
    all_to_all x1, starting transfers between devices, exchange(): return lax.all_to_all(value, 'row', split_axis=0, concat_axis=0, tiled=True)  12.5 us
    all_to_all x1, waiting for transfers between devices, exchange(): return lax.all_to_all(value, 'row', split_axis=0, concat_axis=0, tiled=True)  9.85 us
    ppermute x3, waiting for transfers between devices, shards(): lax.ppermute(own, 'section', [(s, (s + k) % 4) for s in range(4)])  5.15 us
    ppermute x1, waiting for transfers between devices, shards(): taken = lax.ppermute(given, 'section', [(0, 1), (1, 0), (2, 3), (3, 2)])  4.61 us
    ppermute x3, starting transfers between devices, shards(): lax.ppermute(own, 'section', [(s, (s + k) % 4) for s in range(4)])  4.43 us
  transfers between devices with their start and end apart: 5, of which 4 were waited for; matrix products, arithmetic and copies ran while one was open for 0% of the time, Pallas kernels for 3%

profile of v3, /device:TPU:1, one launch (start us, length us, event | category | flops | bytes accessed | tf_op | source)
XLA Modules:
  0.0 185.1 jit_solution(6589045222163852872)
XLA Ops:
  0.0 3.3 %collective-permute-start.2 = (f32[2,16,1024]{2,1,0:T(8,128)}, f32[2,16,1024]{2,1,0:T(8,128)S(1)}, u32[]{:S(2)}, u32[]{:S(2)}) collective-permute-start(f32[2,16,1024]{2,1,0:T(8,128)} %bitcast.40), channel_id=1, source_target_pairs={{0,192},{64,0},{128,64},{192,128},{1,193},{65,1},{129,65},{193,129... | collective-permute-start | bytes 393224 | tf_op jit(solution)/shard_map/ppermute | solution.py:367
  3.3 0.5 collective-permute-start.1
  3.8 0.6 collective-permute-start
  4.4 0.0 copy-start.4
  4.4 3.5 %shard_map.109 = f32[512,128]{1,0:T(8,128)} custom-call(s32[2,2]{1,0:T(2,128)} %offsets_ref.1, f32[2,16,1024]{2,1,0:T(8,128)} %probe_ref.1, f32[2,16,1024]{2,1,0:T(8,128)} %target_ref.1, bf16[128,192]{1,0:T(8,128)(2,1)} %constant.14.clone.ly, f32[2,72,256]{2,1,0:T(8,128)} %constant.15.clone.small, bf16[2,512,512]{2,1,0:T(8,128)(2,1)} %constant.16.clone.ry0), custom_call_target="tpu_custom_call" | custom-call | tf_op jit(solution)/shard_map/pallas_call | solution.py:350
  7.9 0.0 collective-permute-done.2.refs_3_
  7.9 1.0 collective-permute-done.1.refs_2_
  8.9 4.1 %collective-permute-done.refs_1_ = f32[2,16,1024]{2,1,0:T(8,128)S(1)} collective-permute-done((f32[2,16,1024]{2,1,0:T(8,128)}, f32[2,16,1024]{2,1,0:T(8,128)S(1)}, u32[]{:S(2)}, u32[]{:S(2)}) %collective-permute-start) | collective-permute-done | bytes 131104 | tf_op jit(solution)/shard_map/ppermute | solution.py:367
  13.1 0.0 copy-start
  13.1 12.5 %all-to-all-start = ((f32[64,8,128]{2,1,0:T(8,128)}), f32[64,8,128]{2,1,0:T(8,128)S(1)}, u32[]{:S(2)}, u32[]{:S(2)}) async-start(f32[64,8,128]{2,1,0:T(8,128)} %bitcast.44), calls=%async_computation | async-start | bytes 524288 | tf_op jit(solution)/shard_map/all_to_all | solution.py:362
  25.5 0.0 copy-done.4
  25.5 0.0 copy-start.1
  25.6 2.1 %shard_map.110 = (f32[64,512]{1,0:T(8,128)S(1)}, f32[64,512]{1,0:T(8,128)S(1)}, f32[64,512]{1,0:T(8,128)S(1)}, f32[64,512]{1,0:T(8,128)S(1)}) custom-call(f32[2,16,1024]{2,1,0:T(8,128)S(1)} %bitcast.43, f32[2,16,1024]{2,1,0:T(8,128)S(1)} %collective-permute-done.refs_1_, f32[2,16,1024]{2,1,0:T(8,128)S(1)} %collective-permute-done.1.refs_2_, ...), custom_call_target="tpu_custom_call" | custom-call | tf_op jit(solution)/shard_map/pallas_call | solution.py:319
  27.7 9.8 %all-to-all-done = f32[64,8,128]{2,1,0:T(8,128)S(1)} async-done(((f32[64,8,128]{2,1,0:T(8,128)}), f32[64,8,128]{2,1,0:T(8,128)S(1)}, u32[]{:S(2)}, u32[]{:S(2)}) %all-to-all-start) | async-done | bytes 262176 | tf_op jit(solution)/shard_map/all_to_all | solution.py:362
  37.5 0.0 copy-done
  37.5 0.0 copy-done.1
  37.5 0.0 copy-start.3
  37.5 1.3 shard_map.111
  38.8 0.0 copy-start.2
  38.8 18.0 %all_to_all.99 = f32[64,8,128]{2,1,0:T(8,128)S(1)} all-to-all(f32[64,8,128]{2,1,0:T(8,128)S(1)} %bitcast.34), channel_id=1, replica_groups=mesh['section'=4,'row'=64] {'row'}, dimensions={0} | all-to-all | bytes 524288 | tf_op jit(solution)/shard_map/all_to_all | solution.py:362
  56.8 0.0 copy-done.3
  56.8 0.0 copy-done.2
  56.8 1.7 shard_map.112
  58.5 16.2 %all_to_all.100 = f32[64,4,128]{2,1,0:T(4,128)S(1)} all-to-all(f32[64,4,128]{2,1,0:T(4,128)S(1)} %bitcast.38), channel_id=1, replica_groups=mesh['section'=4,'row'=64] {'row'}, dimensions={0} | all-to-all | bytes 262144 | tf_op jit(solution)/shard_map/all_to_all | solution.py:362
  74.7 1.7 shard_map.113
  76.4 16.7 %all_to_all.101 = f32[64,8,128]{2,1,0:T(8,128)S(1)} all-to-all(f32[64,8,128]{2,1,0:T(8,128)S(1)} %bitcast.35), channel_id=1, replica_groups=mesh['section'=4,'row'=64] {'row'}, dimensions={0} | all-to-all | bytes 524288 | tf_op jit(solution)/shard_map/all_to_all | solution.py:362
  93.0 1.2 shard_map.114
  94.3 16.2 %all_to_all.102 = f32[64,4,128]{2,1,0:T(4,128)S(1)} all-to-all(f32[64,4,128]{2,1,0:T(4,128)S(1)} %bitcast.39), channel_id=1, replica_groups=mesh['section'=4,'row'=64] {'row'}, dimensions={0} | all-to-all | bytes 262144 | tf_op jit(solution)/shard_map/all_to_all | solution.py:362
  110.5 0.9 shard_map.115
  111.3 15.0 %all_to_all.103 = f32[64,4,128]{2,1,0:T(4,128)S(1)} all-to-all(f32[64,4,128]{2,1,0:T(4,128)S(1)} %bitcast.33), channel_id=1, replica_groups=mesh['section'=4,'row'=64] {'row'}, dimensions={0} | all-to-all | bytes 262144 | tf_op jit(solution)/shard_map/all_to_all | solution.py:362
  126.4 1.3 shard_map.116
  127.7 15.0 %all_to_all.104 = f32[64,4,128]{2,1,0:T(4,128)S(1)} all-to-all(f32[64,4,128]{2,1,0:T(4,128)S(1)} %bitcast.36), channel_id=1, replica_groups=mesh['section'=4,'row'=64] {'row'}, dimensions={0} | all-to-all | bytes 262144 | tf_op jit(solution)/shard_map/all_to_all | solution.py:362
  142.7 1.7 shard_map.117
  144.4 15.0 %all_to_all.105 = f32[64,4,128]{2,1,0:T(4,128)S(1)} all-to-all(f32[64,4,128]{2,1,0:T(4,128)S(1)} %bitcast.37), channel_id=1, replica_groups=mesh['section'=4,'row'=64] {'row'}, dimensions={0} | all-to-all | bytes 262144 | tf_op jit(solution)/shard_map/all_to_all | solution.py:362
  159.5 1.7 shard_map.118
  161.1 16.7 %all_to_all.106 = f32[64,8,128]{2,1,0:T(8,128)S(1)} all-to-all(f32[64,8,128]{2,1,0:T(8,128)S(1)} %bitcast.27), channel_id=1, replica_groups=mesh['section'=4,'row'=64] {'row'}, dimensions={0} | all-to-all | bytes 524288 | tf_op jit(solution)/shard_map/all_to_all | solution.py:362
  177.8 1.9 %shard_map.119 = (f32[2,16,1024]{2,1,0:T(8,128)S(1)}, f32[2,16,1024]{2,1,0:T(8,128)S(1)}) custom-call(f32[512,128]{1,0:T(8,128)S(1)} %bitcast.26, f32[64,512]{1,0:T(8,128)S(1)} %get-tuple-element.47.refs_1_, f32[64,512]{1,0:T(8,128)S(1)} %get-tuple-element.48.refs_2_, bf16[1024,256]{1,0:T(8,128)(2,1)S(1)} %copy-done, f32[2,136,256]{2,1,0:T(8,128)S(1)} %copy-done.1), custom_call_target="tpu_custom_call" | custom-call | tf_op jit(solution)/shard_map/pallas_call | solution.py:319
  179.7 0.1 collective-permute-start.3
  179.8 4.6 %collective-permute-done.3 = f32[2,16,1024]{2,1,0:T(8,128)S(1)} collective-permute-done((f32[2,16,1024]{2,1,0:T(8,128)S(1)}, f32[2,16,1024]{2,1,0:T(8,128)S(1)}, u32[]{:S(2)}, u32[]{:S(2)}) %collective-permute-start.3) | collective-permute-done | bytes 131104 | tf_op jit(solution)/shard_map/ppermute | solution.py:479
  184.4 0.7 add_bitcast_fusion
Async XLA Ops:
  0.0 7.9 %collective-permute-start.2 = (f32[2,16,1024]{2,1,0:T(8,128)}, f32[2,16,1024]{2,1,0:T(8,128)S(1)}, u32[]{:S(2)}, u32[]{:S(2)}) collective-permute-start(f32[2,16,1024]{2,1,0:T(8,128)} %bitcast.40), channel_id=1, source_target_pairs={{0,192},{64,0},{128,64},{192,128},{1,193},{65,1},{129,65},{193,129... | collective-permute-start | bytes 393224 | tf_op jit(solution)/shard_map/ppermute | solution.py:367
  3.3 5.6 %collective-permute-start.1 = (f32[2,16,1024]{2,1,0:T(8,128)}, f32[2,16,1024]{2,1,0:T(8,128)S(1)}, u32[]{:S(2)}, u32[]{:S(2)}) collective-permute-start(f32[2,16,1024]{2,1,0:T(8,128)} %bitcast.41), channel_id=1, source_target_pairs={{0,128},{64,192},{128,0},{192,64},{1,129},{65,193},{129,1},{193,65... | collective-permute-start | bytes 393224 | tf_op jit(solution)/shard_map/ppermute | solution.py:367
  3.8 9.2 %collective-permute-start = (f32[2,16,1024]{2,1,0:T(8,128)}, f32[2,16,1024]{2,1,0:T(8,128)S(1)}, u32[]{:S(2)}, u32[]{:S(2)}) collective-permute-start(f32[2,16,1024]{2,1,0:T(8,128)} %bitcast.42), channel_id=1, source_target_pairs={{0,64},{64,128},{128,192},{192,0},{1,65},{65,129},{129,193},{193,1... | collective-permute-start | bytes 393224 | tf_op jit(solution)/shard_map/ppermute | solution.py:367
  4.4 21.1 %copy-start.4 = (f32[1,2,16,1024]{3,2,1,0:T(8,128)S(1)}, f32[1,2,16,1024]{3,2,1,0:T(8,128)}, u32[]{:S(2)}) copy-start(f32[1,2,16,1024]{3,2,1,0:T(8,128)} %param.11) | copy-start | bytes 393220
  13.1 24.5 %copy-start = (bf16[1024,256]{1,0:T(8,128)(2,1)S(1)}, bf16[1024,256]{1,0:T(8,128)(2,1)}, u32[]{:S(2)}) copy-start(bf16[1024,256]{1,0:T(8,128)(2,1)} %constant.17.clone.refs_3_.refs_2_) | copy-start | bytes 1572868
  13.1 24.5 %all-to-all-start = ((f32[64,8,128]{2,1,0:T(8,128)}), f32[64,8,128]{2,1,0:T(8,128)S(1)}, u32[]{:S(2)}, u32[]{:S(2)}) async-start(f32[64,8,128]{2,1,0:T(8,128)} %bitcast.44), calls=%async_computation | async-start | bytes 524288 | tf_op jit(solution)/shard_map/all_to_all | solution.py:362
  25.5 12.0 %copy-start.1 = (f32[2,136,256]{2,1,0:T(8,128)S(1)}, f32[2,136,256]{2,1,0:T(8,128)}, u32[]{:S(2)}) copy-start(f32[2,136,256]{2,1,0:T(8,128)} %constant.18.clone.refs_4_.refs_3_) | copy-start | bytes 835588
  37.5 19.3 %copy-start.3 = (f32[2,136,256]{2,1,0:T(8,128)S(1)}, f32[2,136,256]{2,1,0:T(8,128)}, u32[]{:S(2)}) copy-start(f32[2,136,256]{2,1,0:T(8,128)} %constant.20.clone.refs_2_.refs_4_.refs_5_) | copy-start | bytes 835588
  38.8 18.0 %copy-start.2 = (bf16[640,256]{1,0:T(8,128)(2,1)S(1)}, bf16[640,256]{1,0:T(8,128)(2,1)}, u32[]{:S(2)}) copy-start(bf16[640,256]{1,0:T(8,128)(2,1)} %constant.19.clone.refs_1_.refs_3_.refs_4_) | copy-start | bytes 983044
  179.7 4.7 %collective-permute-start.3 = (f32[2,16,1024]{2,1,0:T(8,128)S(1)}, f32[2,16,1024]{2,1,0:T(8,128)S(1)}, u32[]{:S(2)}, u32[]{:S(2)}) collective-permute-start(f32[2,16,1024]{2,1,0:T(8,128)S(1)} %get-tuple-element.50), channel_id=1, source_target_pairs={{0,64},{64,0},{128,192},{192,128},{1,65},{65,1},{129,193},{193,129... | collective-permute-start | bytes 393224 | tf_op jit(solution)/shard_map/ppermute | solution.py:479

commit v4 on v3

--- a/solution.py
+++ b/solution.py
@@ -100,11 +100,12 @@
     return {
         "y16": rows([tab["ly"], tab["ry"][0], tab["ry"][1]]),
         "y32": both(("ty", "hy", "by")),
-        "x16": rows([tab["lxf"], tab["lxi"], tab["rx"][0], tab["rx"][1], tab["pm"]]),
+        "x16": rows([tab["lxf"], tab["lxi"], tab["rx"][0], tab["rx"][1]]),
         "x32": both(("tx", "hx", "bx")),
         "first32": both(("ty", "by0")),
         "ry0": tab["ry0"],
         "ly": tab["ly"],
+        "pm": tab["pm"],
     }
 
 
@@ -243,7 +244,6 @@
     else:
         tab["lxf"], tab["lxi"] = small[0:128, 0:192], small[128:256, 0:192]
         tab["rx"] = (small[256:512, :], small[512:768, :])
-        tab["pm"] = small[768:1024, :]
     for name, at, lanes in (("t", slice(0, 64), L), ("h", slice(64, 128), L)):
         tab[name + axis] = tuple(large[part, at, 0:lanes] for part in range(2))
     lanes = L if axis == "y" else 128
@@ -287,7 +287,7 @@
     spec = rows_join(*y_unfold(spec, tab["by0"]))
     out = times(jnp.concatenate(spec, axis=1), tab["ry0"])
     field = left(tab["ly"], mul((out[:, :L], out[:, L:]), tab["ty"]), -1)
-    return jnp.concatenate(field + (spread(target), jnp.zeros((B, L), f32)), axis=1)
+    return jnp.concatenate(field + (lanes_permuted(spread(target), tab["pm"]),), axis=1)
 
 
 def forward_of(axis):
@@ -326,11 +326,11 @@
 
 
 def first_call(probe, target, offsets):
-    names = ("ly", "first32", "ry0")
-
-    def kernel(offsets_ref, probe_ref, target_ref, ly, small, ry0, out):
+    names = ("ly", "pm", "first32", "ry0")
+
+    def kernel(offsets_ref, probe_ref, target_ref, ly, pm, small, ry0, out):
         wave = lax.axis_index("section") % 2
-        tab = {"ly": ly[...], "ry0": (ry0[0], ry0[1])}
+        tab = {"ly": ly[...], "pm": pm[...], "ry0": (ry0[0], ry0[1])}
         tab["ty"] = (small[0, 0:64], small[1, 0:64])
         tab["by0"] = (small[0, 64:72], small[1, 64:72])
         ramp = ramp_of(offsets_ref[wave, 0], offsets_ref[wave, 1], lax.axis_index("row"))
@@ -350,10 +350,10 @@
     return pl.pallas_call(
         kernel,
         grid=(1,),
-        out_shape=jax.ShapeDtypeStruct((8 * B, 128), f32),
+        out_shape=jax.ShapeDtypeStruct((6 * B, 128), f32),
         in_specs=[pl.BlockSpec((2, 2), lambda i: (0, 0), memory_space=pltpu.SMEM)]
         + [whole(a.shape) for a in arrays],
-        out_specs=whole((8 * B, 128)),
+        out_specs=whole((6 * B, 128)),
         compiler_params=pltpu.CompilerParams(vmem_limit_bytes=FIRST_LIMIT),
     )(offsets, *arrays)
 
@@ -366,7 +366,7 @@
     own = object_slices[0]
     raw = [lax.ppermute(own, "section", [(s, (s + k) % 4) for s in range(4)]) for k in (1, 2, 3)]
     sent, *raw = lax.optimization_barrier((first_call(probe_spec, measured, offsets), *raw))
-    got1 = exchange(sent)
+    got1 = exchange(sent.reshape(B, 1, 3 * L)).reshape(6 * B, 128)
 
     def arrange(tab, ins, outs):
         place = lax.axis_index("section")
@@ -386,7 +386,7 @@
         outs[0][...] = jnp.concatenate(psi, axis=1)
         a = propagate("x", mul(psi, parts_of(ins[1][...])), tab, False)
         put(outs[1], jnp.concatenate(a + (ins[2][...],), axis=1))
-        outs[2][...] = lanes_permuted(value[:, 2 * L : 3 * L], tab["pm"])
+        outs[2][...] = value[:, 2 * L :]
 
     psi0, sent, target = call(
         second,
@@ -472,11 +472,17 @@
         upper = parts_of(value, 2 * L)
         for part in range(2):
             lower = jnp.where(pos < 2, grad[part], other[part])
-            outs[0][part] = collect(jnp.where(pos % 2 == 0, lower, upper[part]))
-            outs[1][part] = collect(jnp.where(pos % 2 == 0, upper[part], lower))
-
-    kept, given = call(last, "x", (exchange(sent), psi0, grad2), ((2, T, N),) * 2)
+            outs[0][part] = collect(jnp.where(pos % 2 == 0, upper[part], lower))
+            outs[1][:, part * L : part * L + L] = jnp.where(pos % 2 == 0, lower, upper[part])
+
+    given, kept = call(last, "x", (exchange(sent), psi0, grad2), ((2, T, N), (B, 2 * L)))
     taken = lax.ppermute(given, "section", [(0, 1), (1, 0), (2, 3), (3, 2)])
+
+    def lay_out(tab, ins, outs):
+        for part in range(2):
+            outs[0][part] = collect(ins[0][:, part * L : part * L + L])
+
+    (kept,) = call(lay_out, "", (kept,), ((2, T, N),))
     return (kept + taken)[None]
 
 

time: 186 us -> 184 us (0.989)
    pallas_call x10 -> x11, Pallas kernels: 15.4 us -> 15.4 us  [call(): pl.pallas_call(kernel, out_shape=[jax.ShapeDtypeStruct(shape, f32) for sh...]
where the time goes in v4:
time: 184 us; the launch traced here: 183 us
  blocking collectives  128 us (70%)
  Pallas kernels  19 us (10%)
  waiting for transfers between devices  18 us (10%)
  starting transfers between devices  17 us (9%)
    all_to_all x8, blocking collectives, exchange(): return lax.all_to_all(value, 'row', split_axis=0, concat_axis=0, tiled=True)  128 us
    pallas_call x11, Pallas kernels, call(): pl.pallas_call(kernel, out_shape=[jax.ShapeDtypeStruct(shape, f32) for sh...  15.4 us
    all_to_all x1, starting transfers between devices, exchange(): return lax.all_to_all(value, 'row', split_axis=0, concat_axis=0, tiled=True)  12.5 us
    all_to_all x1, waiting for transfers between devices, exchange(): return lax.all_to_all(value, 'row', split_axis=0, concat_axis=0, tiled=True)  8.78 us
    ppermute x3, waiting for transfers between devices, shards(): lax.ppermute(own, 'section', [(s, (s + k) % 4) for s in range(4)])  5.11 us
    ppermute x3, starting transfers between devices, shards(): lax.ppermute(own, 'section', [(s, (s + k) % 4) for s in range(4)])  4.43 us
    ppermute x1, waiting for transfers between devices, shards(): taken = lax.ppermute(given, 'section', [(0, 1), (1, 0), (2, 3), (3, 2)])  4.06 us
  transfers between devices with their start and end apart: 5, of which 4 were waited for; matrix products, arithmetic and copies ran while one was open for 0% of the time, Pallas kernels for 3%

profile of v4, /device:TPU:1, one launch (start us, length us, event | category | flops | bytes accessed | tf_op | source)
XLA Modules:
  0.0 183.2 jit_solution(3623751336172967132)
XLA Ops:
  0.0 3.3 %collective-permute-start.2 = (f32[2,16,1024]{2,1,0:T(8,128)}, f32[2,16,1024]{2,1,0:T(8,128)S(1)}, u32[]{:S(2)}, u32[]{:S(2)}) collective-permute-start(f32[2,16,1024]{2,1,0:T(8,128)} %bitcast.40), channel_id=1, source_target_pairs={{0,192},{64,0},{128,64},{192,128},{1,193},{65,1},{129,65},{193,129... | collective-permute-start | bytes 393224 | tf_op jit(solution)/shard_map/ppermute | solution.py:367
  3.3 0.5 collective-permute-start.1
  3.8 0.6 collective-permute-start
  4.4 0.0 copy-start.4
  4.4 3.5 %shard_map.118 = f32[384,128]{1,0:T(8,128)} custom-call(s32[2,2]{1,0:T(2,128)} %offsets_ref.1, f32[2,16,1024]{2,1,0:T(8,128)} %probe_ref.1, f32[2,16,1024]{2,1,0:T(8,128)} %target_ref.1, bf16[128,192]{1,0:T(8,128)(2,1)} %constant.16.clone.ly, bf16[256,256]{1,0:T(8,128)(2,1)} %constant.17.clone.pm, f32[2,72,256]{2,1,0:T(8,128)} %constant.18.clone.small, ...), custom_call_target="tpu_custom_call" | custom-call | tf_op jit(solution)/shard_map/pallas_call | solution.py:350
  7.9 0.0 collective-permute-done.2.refs_3_
  7.9 1.0 collective-permute-done.1.refs_2_
  8.9 4.1 %collective-permute-done.refs_1_ = f32[2,16,1024]{2,1,0:T(8,128)S(1)} collective-permute-done((f32[2,16,1024]{2,1,0:T(8,128)}, f32[2,16,1024]{2,1,0:T(8,128)S(1)}, u32[]{:S(2)}, u32[]{:S(2)}) %collective-permute-start) | collective-permute-done | bytes 131104 | tf_op jit(solution)/shard_map/ppermute | solution.py:367
  13.1 0.0 copy-start
  13.1 12.5 %all-to-all-start = ((f32[64,1,768]{2,1,0:T(1,128)}), f32[64,1,768]{2,1,0:T(1,128)S(1)}, u32[]{:S(2)}, u32[]{:S(2)}) async-start(f32[64,1,768]{2,1,0:T(1,128)} %bitcast.44), calls=%async_computation | async-start | bytes 393216 | tf_op jit(solution)/shard_map/all_to_all | solution.py:362
  25.5 0.0 copy-done.4
  25.5 0.0 copy-start.1
  25.6 2.1 %shard_map.119 = (f32[64,512]{1,0:T(8,128)S(1)}, f32[64,512]{1,0:T(8,128)S(1)}, f32[64,512]{1,0:T(8,128)S(1)}, f32[64,512]{1,0:T(8,128)S(1)}) custom-call(f32[2,16,1024]{2,1,0:T(8,128)S(1)} %bitcast.43, f32[2,16,1024]{2,1,0:T(8,128)S(1)} %collective-permute-done.refs_1_, f32[2,16,1024]{2,1,0:T(8,128)S(1)} %collective-permute-done.1.refs_2_, ...), custom_call_target="tpu_custom_call" | custom-call | tf_op jit(solution)/shard_map/pallas_call | solution.py:319
  27.7 8.8 %all-to-all-done = f32[64,1,768]{2,1,0:T(1,128)S(1)} async-done(((f32[64,1,768]{2,1,0:T(1,128)}), f32[64,1,768]{2,1,0:T(1,128)S(1)}, u32[]{:S(2)}, u32[]{:S(2)}) %all-to-all-start) | async-done | bytes 196640 | tf_op jit(solution)/shard_map/all_to_all | solution.py:362
  36.5 0.0 copy-done
  36.5 0.0 copy-done.1
  36.5 0.0 copy-start.3
  36.5 1.3 shard_map.120
  37.8 0.0 copy-start.2
  37.8 17.6 %all_to_all.93 = f32[64,8,128]{2,1,0:T(8,128)S(1)} all-to-all(f32[64,8,128]{2,1,0:T(8,128)S(1)} %bitcast.34), channel_id=1, replica_groups=mesh['section'=4,'row'=64] {'row'}, dimensions={0} | all-to-all | bytes 524288 | tf_op jit(solution)/shard_map/all_to_all | solution.py:362
  55.4 0.0 copy-done.3
  55.4 0.0 copy-done.2
  55.4 1.7 shard_map.121
  57.1 16.2 %all_to_all.94 = f32[64,4,128]{2,1,0:T(4,128)S(1)} all-to-all(f32[64,4,128]{2,1,0:T(4,128)S(1)} %bitcast.38), channel_id=1, replica_groups=mesh['section'=4,'row'=64] {'row'}, dimensions={0} | all-to-all | bytes 262144 | tf_op jit(solution)/shard_map/all_to_all | solution.py:362
  73.3 1.7 shard_map.122
  75.0 16.7 %all_to_all.95 = f32[64,8,128]{2,1,0:T(8,128)S(1)} all-to-all(f32[64,8,128]{2,1,0:T(8,128)S(1)} %bitcast.35), channel_id=1, replica_groups=mesh['section'=4,'row'=64] {'row'}, dimensions={0} | all-to-all | bytes 524288 | tf_op jit(solution)/shard_map/all_to_all | solution.py:362
  91.6 1.2 shard_map.123
  92.9 16.2 %all_to_all.96 = f32[64,4,128]{2,1,0:T(4,128)S(1)} all-to-all(f32[64,4,128]{2,1,0:T(4,128)S(1)} %bitcast.39), channel_id=1, replica_groups=mesh['section'=4,'row'=64] {'row'}, dimensions={0} | all-to-all | bytes 262144 | tf_op jit(solution)/shard_map/all_to_all | solution.py:362
  109.1 0.9 shard_map.124
  109.9 15.0 %all_to_all.97 = f32[64,4,128]{2,1,0:T(4,128)S(1)} all-to-all(f32[64,4,128]{2,1,0:T(4,128)S(1)} %bitcast.31), channel_id=1, replica_groups=mesh['section'=4,'row'=64] {'row'}, dimensions={0} | all-to-all | bytes 262144 | tf_op jit(solution)/shard_map/all_to_all | solution.py:362
  125.0 1.3 shard_map.125
  126.3 15.0 %all_to_all.98 = f32[64,4,128]{2,1,0:T(4,128)S(1)} all-to-all(f32[64,4,128]{2,1,0:T(4,128)S(1)} %bitcast.36), channel_id=1, replica_groups=mesh['section'=4,'row'=64] {'row'}, dimensions={0} | all-to-all | bytes 262144 | tf_op jit(solution)/shard_map/all_to_all | solution.py:362
  141.3 1.7 shard_map.126
  143.0 15.0 %all_to_all.99 = f32[64,4,128]{2,1,0:T(4,128)S(1)} all-to-all(f32[64,4,128]{2,1,0:T(4,128)S(1)} %bitcast.37), channel_id=1, replica_groups=mesh['section'=4,'row'=64] {'row'}, dimensions={0} | all-to-all | bytes 262144 | tf_op jit(solution)/shard_map/all_to_all | solution.py:362
  158.1 1.7 shard_map.127
  159.7 16.7 %all_to_all.100 = f32[64,8,128]{2,1,0:T(8,128)S(1)} all-to-all(f32[64,8,128]{2,1,0:T(8,128)S(1)} %bitcast.26), channel_id=1, replica_groups=mesh['section'=4,'row'=64] {'row'}, dimensions={0} | all-to-all | bytes 524288 | tf_op jit(solution)/shard_map/all_to_all | solution.py:362
  176.4 1.4 shard_map.128
  177.8 0.1 collective-permute-start.3
  177.9 0.6 shard_map.129
  178.5 4.1 %collective-permute-done.3 = f32[2,16,1024]{2,1,0:T(8,128)S(1)} collective-permute-done((f32[2,16,1024]{2,1,0:T(8,128)S(1)}, f32[2,16,1024]{2,1,0:T(8,128)S(1)}, u32[]{:S(2)}, u32[]{:S(2)}) %collective-permute-start.3) | collective-permute-done | bytes 131104 | tf_op jit(solution)/shard_map/ppermute | solution.py:479
  182.5 0.7 add_bitcast_fusion
Async XLA Ops:
  0.0 7.9 %collective-permute-start.2 = (f32[2,16,1024]{2,1,0:T(8,128)}, f32[2,16,1024]{2,1,0:T(8,128)S(1)}, u32[]{:S(2)}, u32[]{:S(2)}) collective-permute-start(f32[2,16,1024]{2,1,0:T(8,128)} %bitcast.40), channel_id=1, source_target_pairs={{0,192},{64,0},{128,64},{192,128},{1,193},{65,1},{129,65},{193,129... | collective-permute-start | bytes 393224 | tf_op jit(solution)/shard_map/ppermute | solution.py:367
  3.3 5.6 %collective-permute-start.1 = (f32[2,16,1024]{2,1,0:T(8,128)}, f32[2,16,1024]{2,1,0:T(8,128)S(1)}, u32[]{:S(2)}, u32[]{:S(2)}) collective-permute-start(f32[2,16,1024]{2,1,0:T(8,128)} %bitcast.41), channel_id=1, source_target_pairs={{0,128},{64,192},{128,0},{192,64},{1,129},{65,193},{129,1},{193,65... | collective-permute-start | bytes 393224 | tf_op jit(solution)/shard_map/ppermute | solution.py:367
  3.8 9.2 %collective-permute-start = (f32[2,16,1024]{2,1,0:T(8,128)}, f32[2,16,1024]{2,1,0:T(8,128)S(1)}, u32[]{:S(2)}, u32[]{:S(2)}) collective-permute-start(f32[2,16,1024]{2,1,0:T(8,128)} %bitcast.42), channel_id=1, source_target_pairs={{0,64},{64,128},{128,192},{192,0},{1,65},{65,129},{129,193},{193,1... | collective-permute-start | bytes 393224 | tf_op jit(solution)/shard_map/ppermute | solution.py:367
  4.4 21.1 %copy-start.4 = (f32[1,2,16,1024]{3,2,1,0:T(8,128)S(1)}, f32[1,2,16,1024]{3,2,1,0:T(8,128)}, u32[]{:S(2)}) copy-start(f32[1,2,16,1024]{3,2,1,0:T(8,128)} %param.12) | copy-start | bytes 393220
  13.1 23.4 %copy-start = (bf16[768,256]{1,0:T(8,128)(2,1)S(1)}, bf16[768,256]{1,0:T(8,128)(2,1)}, u32[]{:S(2)}) copy-start(bf16[768,256]{1,0:T(8,128)(2,1)} %constant.20.clone.refs_3_.refs_2_) | copy-start | bytes 1179652
  13.1 23.4 %all-to-all-start = ((f32[64,1,768]{2,1,0:T(1,128)}), f32[64,1,768]{2,1,0:T(1,128)S(1)}, u32[]{:S(2)}, u32[]{:S(2)}) async-start(f32[64,1,768]{2,1,0:T(1,128)} %bitcast.44), calls=%async_computation | async-start | bytes 393216 | tf_op jit(solution)/shard_map/all_to_all | solution.py:362
  25.5 10.9 %copy-start.1 = (f32[2,136,256]{2,1,0:T(8,128)S(1)}, f32[2,136,256]{2,1,0:T(8,128)}, u32[]{:S(2)}) copy-start(f32[2,136,256]{2,1,0:T(8,128)} %constant.21.clone.refs_4_.refs_3_) | copy-start | bytes 835588
  36.5 18.9 %copy-start.3 = (f32[2,136,256]{2,1,0:T(8,128)S(1)}, f32[2,136,256]{2,1,0:T(8,128)}, u32[]{:S(2)}) copy-start(f32[2,136,256]{2,1,0:T(8,128)} %constant.23.clone.refs_2_.refs_4_.refs_5_) | copy-start | bytes 835588
  37.8 17.6 %copy-start.2 = (bf16[640,256]{1,0:T(8,128)(2,1)S(1)}, bf16[640,256]{1,0:T(8,128)(2,1)}, u32[]{:S(2)}) copy-start(bf16[640,256]{1,0:T(8,128)(2,1)} %constant.22.clone.refs_1_.refs_3_.refs_4_) | copy-start | bytes 983044
  177.8 4.7 %collective-permute-start.3 = (f32[2,16,1024]{2,1,0:T(8,128)S(1)}, f32[2,16,1024]{2,1,0:T(8,128)S(1)}, u32[]{:S(2)}, u32[]{:S(2)}) collective-permute-start(f32[2,16,1024]{2,1,0:T(8,128)S(1)} %get-tuple-element.50), channel_id=1, source_target_pairs={{0,64},{64,0},{128,192},{192,128},{1,65},{65,1},{129,193},{193,129... | collective-permute-start | bytes 393224 | tf_op jit(solution)/shard_map/ppermute | solution.py:479

commit v5 on v4

--- a/solution.py
+++ b/solution.py
@@ -364,8 +364,14 @@
 
 def shards(object_slices, probe_spec, offsets, measured):
     own = object_slices[0]
-    raw = [lax.ppermute(own, "section", [(s, (s + k) % 4) for s in range(4)]) for k in (1, 2, 3)]
-    sent, *raw = lax.optimization_barrier((first_call(probe_spec, measured, offsets), *raw))
+    def moved(k):
+        return lax.ppermute(own, "section", [(s, (s + k) % 4) for s in range(4)])
+
+    behind, ahead, across = moved(3), moved(1), moved(2)
+    sent, behind, ahead, across = lax.optimization_barrier(
+        (first_call(probe_spec, measured, offsets), behind, ahead, across)
+    )
+    raw = (ahead, across, behind)
     got1 = exchange(sent.reshape(B, 1, 3 * L)).reshape(6 * B, 128)
 
     def arrange(tab, ins, outs):

time: 184 us -> 182 us (0.989)
  waiting for transfers between devices: 18 us -> 13.1 us
  starting transfers between devices: 17 us -> 19.7 us
    ppermute x3, waiting for transfers between devices: 5.11 us -> 1.23 us  [moved(): return lax.ppermute(own, 'section', [(s, (s + k) % 4) for s in range(4)])]
  transfers between devices with their start and end apart: 5 -> 5, of which waited for: 4 -> 3; matrix products, arithmetic and copies ran while one was open for 0% -> 0% of each run, Pallas kernels for 3% -> 3%
where the time goes in v5:
time: 182 us; the launch traced here: 181 us
  blocking collectives  128 us (70%)
  starting transfers between devices  19.7 us (11%)
  Pallas kernels  19 us (10%)
  waiting for transfers between devices  13.1 us (7%)
    all_to_all x8, blocking collectives, exchange(): return lax.all_to_all(value, 'row', split_axis=0, concat_axis=0, tiled=True)  128 us
    pallas_call x11, Pallas kernels, call(): pl.pallas_call(kernel, out_shape=[jax.ShapeDtypeStruct(shape, f32) for sh...  15.4 us
    all_to_all x1, starting transfers between devices, exchange(): return lax.all_to_all(value, 'row', split_axis=0, concat_axis=0, tiled=True)  12.4 us
    all_to_all x1, waiting for transfers between devices, exchange(): return lax.all_to_all(value, 'row', split_axis=0, concat_axis=0, tiled=True)  8.78 us
    ppermute x3, starting transfers between devices, moved(): return lax.ppermute(own, 'section', [(s, (s + k) % 4) for s in range(4)])  6.25 us
  transfers between devices with their start and end apart: 5, of which 3 were waited for; matrix products, arithmetic and copies ran while one was open for 0% of the time, Pallas kernels for 3%

profile of v5, /device:TPU:1, one launch (start us, length us, event | category | flops | bytes accessed | tf_op | source)
XLA Modules:
  0.0 181.1 jit_solution(16931318072528620754)
XLA Ops:
  0.0 3.6 %collective-permute-start.2 = (f32[2,16,1024]{2,1,0:T(8,128)}, f32[2,16,1024]{2,1,0:T(8,128)S(1)}, u32[]{:S(2)}, u32[]{:S(2)}) collective-permute-start(f32[2,16,1024]{2,1,0:T(8,128)} %bitcast.40), channel_id=1, source_target_pairs={{0,128},{64,192},{128,0},{192,64},{1,129},{65,193},{129,1},{193,65... | collective-permute-start | bytes 393224 | tf_op jit(solution)/shard_map/ppermute | solution.py:368
  3.6 0.3 collective-permute-start.1
  3.9 2.4 %collective-permute-start = (f32[2,16,1024]{2,1,0:T(8,128)}, f32[2,16,1024]{2,1,0:T(8,128)S(1)}, u32[]{:S(2)}, u32[]{:S(2)}) collective-permute-start(f32[2,16,1024]{2,1,0:T(8,128)} %bitcast.42), channel_id=1, source_target_pairs={{0,192},{64,0},{128,64},{192,128},{1,193},{65,1},{129,65},{193,129... | collective-permute-start | bytes 393224 | tf_op jit(solution)/shard_map/ppermute | solution.py:368
  6.3 0.0 copy-start.4
  6.3 3.5 %shard_map.118 = f32[384,128]{1,0:T(8,128)} custom-call(s32[2,2]{1,0:T(2,128)} %offsets_ref.1, f32[2,16,1024]{2,1,0:T(8,128)} %probe_ref.1, f32[2,16,1024]{2,1,0:T(8,128)} %target_ref.1, bf16[128,192]{1,0:T(8,128)(2,1)} %constant.16.clone.ly, bf16[256,256]{1,0:T(8,128)(2,1)} %constant.17.clone.pm, f32[2,72,256]{2,1,0:T(8,128)} %constant.18.clone.small, ...), custom_call_target="tpu_custom_call" | custom-call | tf_op jit(solution)/shard_map/pallas_call | solution.py:350
  9.8 0.0 collective-permute-done.2.refs_2_
  9.8 1.2 collective-permute-done.1.refs_1_
  11.0 0.0 collective-permute-done.refs_3_
  11.0 0.0 copy-start
  11.0 12.4 %all-to-all-start = ((f32[64,1,768]{2,1,0:T(1,128)}), f32[64,1,768]{2,1,0:T(1,128)S(1)}, u32[]{:S(2)}, u32[]{:S(2)}) async-start(f32[64,1,768]{2,1,0:T(1,128)} %bitcast.44), calls=%async_computation | async-start | bytes 393216 | tf_op jit(solution)/shard_map/all_to_all | solution.py:362
  23.4 0.0 copy-done.4
  23.4 0.0 copy-start.1
  23.4 2.1 %shard_map.119 = (f32[64,512]{1,0:T(8,128)S(1)}, f32[64,512]{1,0:T(8,128)S(1)}, f32[64,512]{1,0:T(8,128)S(1)}, f32[64,512]{1,0:T(8,128)S(1)}) custom-call(f32[2,16,1024]{2,1,0:T(8,128)S(1)} %bitcast.43, f32[2,16,1024]{2,1,0:T(8,128)S(1)} %collective-permute-done.1.refs_1_, f32[2,16,1024]{2,1,0:T(8,128)S(1)} %collective-permute-done.2.refs_2_, ...), custom_call_target="tpu_custom_call" | custom-call | tf_op jit(solution)/shard_map/pallas_call | solution.py:319
  25.6 8.8 %all-to-all-done = f32[64,1,768]{2,1,0:T(1,128)S(1)} async-done(((f32[64,1,768]{2,1,0:T(1,128)}), f32[64,1,768]{2,1,0:T(1,128)S(1)}, u32[]{:S(2)}, u32[]{:S(2)}) %all-to-all-start) | async-done | bytes 196640 | tf_op jit(solution)/shard_map/all_to_all | solution.py:362
  34.3 0.0 copy-done
  34.3 0.0 copy-done.1
  34.3 0.0 copy-start.3
  34.3 1.3 shard_map.120
  35.6 0.0 copy-start.2
  35.6 17.6 %all_to_all.93 = f32[64,8,128]{2,1,0:T(8,128)S(1)} all-to-all(f32[64,8,128]{2,1,0:T(8,128)S(1)} %bitcast.34), channel_id=1, replica_groups=mesh['section'=4,'row'=64] {'row'}, dimensions={0} | all-to-all | bytes 524288 | tf_op jit(solution)/shard_map/all_to_all | solution.py:362
  53.3 0.0 copy-done.3
  53.3 0.0 copy-done.2
  53.3 1.7 shard_map.121
  54.9 16.2 %all_to_all.94 = f32[64,4,128]{2,1,0:T(4,128)S(1)} all-to-all(f32[64,4,128]{2,1,0:T(4,128)S(1)} %bitcast.38), channel_id=1, replica_groups=mesh['section'=4,'row'=64] {'row'}, dimensions={0} | all-to-all | bytes 262144 | tf_op jit(solution)/shard_map/all_to_all | solution.py:362
  71.1 1.7 shard_map.122
  72.8 16.7 %all_to_all.95 = f32[64,8,128]{2,1,0:T(8,128)S(1)} all-to-all(f32[64,8,128]{2,1,0:T(8,128)S(1)} %bitcast.35), channel_id=1, replica_groups=mesh['section'=4,'row'=64] {'row'}, dimensions={0} | all-to-all | bytes 524288 | tf_op jit(solution)/shard_map/all_to_all | solution.py:362
  89.5 1.2 shard_map.123
  90.8 16.2 %all_to_all.96 = f32[64,4,128]{2,1,0:T(4,128)S(1)} all-to-all(f32[64,4,128]{2,1,0:T(4,128)S(1)} %bitcast.39), channel_id=1, replica_groups=mesh['section'=4,'row'=64] {'row'}, dimensions={0} | all-to-all | bytes 262144 | tf_op jit(solution)/shard_map/all_to_all | solution.py:362
  106.9 0.9 shard_map.124
  107.8 15.0 %all_to_all.97 = f32[64,4,128]{2,1,0:T(4,128)S(1)} all-to-all(f32[64,4,128]{2,1,0:T(4,128)S(1)} %bitcast.31), channel_id=1, replica_groups=mesh['section'=4,'row'=64] {'row'}, dimensions={0} | all-to-all | bytes 262144 | tf_op jit(solution)/shard_map/all_to_all | solution.py:362
  122.9 1.3 shard_map.125
  124.1 15.0 %all_to_all.98 = f32[64,4,128]{2,1,0:T(4,128)S(1)} all-to-all(f32[64,4,128]{2,1,0:T(4,128)S(1)} %bitcast.36), channel_id=1, replica_groups=mesh['section'=4,'row'=64] {'row'}, dimensions={0} | all-to-all | bytes 262144 | tf_op jit(solution)/shard_map/all_to_all | solution.py:362
  139.2 1.7 shard_map.126
  140.9 15.0 %all_to_all.99 = f32[64,4,128]{2,1,0:T(4,128)S(1)} all-to-all(f32[64,4,128]{2,1,0:T(4,128)S(1)} %bitcast.37), channel_id=1, replica_groups=mesh['section'=4,'row'=64] {'row'}, dimensions={0} | all-to-all | bytes 262144 | tf_op jit(solution)/shard_map/all_to_all | solution.py:362
  155.9 1.7 shard_map.127
  157.6 16.7 %all_to_all.100 = f32[64,8,128]{2,1,0:T(8,128)S(1)} all-to-all(f32[64,8,128]{2,1,0:T(8,128)S(1)} %bitcast.26), channel_id=1, replica_groups=mesh['section'=4,'row'=64] {'row'}, dimensions={0} | all-to-all | bytes 524288 | tf_op jit(solution)/shard_map/all_to_all | solution.py:362
  174.3 1.4 shard_map.128
  175.7 1.0 collective-permute-start.3
  176.7 0.6 shard_map.129
  177.3 3.1 %collective-permute-done.3 = f32[2,16,1024]{2,1,0:T(8,128)S(1)} collective-permute-done((f32[2,16,1024]{2,1,0:T(8,128)S(1)}, f32[2,16,1024]{2,1,0:T(8,128)S(1)}, u32[]{:S(2)}, u32[]{:S(2)}) %collective-permute-start.3) | collective-permute-done | bytes 131104 | tf_op jit(solution)/shard_map/ppermute | solution.py:485
  180.4 0.7 add_bitcast_fusion
Async XLA Ops:
  0.0 9.8 %collective-permute-start.2 = (f32[2,16,1024]{2,1,0:T(8,128)}, f32[2,16,1024]{2,1,0:T(8,128)S(1)}, u32[]{:S(2)}, u32[]{:S(2)}) collective-permute-start(f32[2,16,1024]{2,1,0:T(8,128)} %bitcast.40), channel_id=1, source_target_pairs={{0,128},{64,192},{128,0},{192,64},{1,129},{65,193},{129,1},{193,65... | collective-permute-start | bytes 393224 | tf_op jit(solution)/shard_map/ppermute | solution.py:368
  3.6 7.4 %collective-permute-start.1 = (f32[2,16,1024]{2,1,0:T(8,128)}, f32[2,16,1024]{2,1,0:T(8,128)S(1)}, u32[]{:S(2)}, u32[]{:S(2)}) collective-permute-start(f32[2,16,1024]{2,1,0:T(8,128)} %bitcast.41), channel_id=1, source_target_pairs={{0,64},{64,128},{128,192},{192,0},{1,65},{65,129},{129,193},{193,1... | collective-permute-start | bytes 393224 | tf_op jit(solution)/shard_map/ppermute | solution.py:368
  3.9 7.1 %collective-permute-start = (f32[2,16,1024]{2,1,0:T(8,128)}, f32[2,16,1024]{2,1,0:T(8,128)S(1)}, u32[]{:S(2)}, u32[]{:S(2)}) collective-permute-start(f32[2,16,1024]{2,1,0:T(8,128)} %bitcast.42), channel_id=1, source_target_pairs={{0,192},{64,0},{128,64},{192,128},{1,193},{65,1},{129,65},{193,129... | collective-permute-start | bytes 393224 | tf_op jit(solution)/shard_map/ppermute | solution.py:368
  6.3 17.2 %copy-start.4 = (f32[1,2,16,1024]{3,2,1,0:T(8,128)S(1)}, f32[1,2,16,1024]{3,2,1,0:T(8,128)}, u32[]{:S(2)}) copy-start(f32[1,2,16,1024]{3,2,1,0:T(8,128)} %param.12) | copy-start | bytes 393220
  11.0 23.3 %copy-start = (bf16[768,256]{1,0:T(8,128)(2,1)S(1)}, bf16[768,256]{1,0:T(8,128)(2,1)}, u32[]{:S(2)}) copy-start(bf16[768,256]{1,0:T(8,128)(2,1)} %constant.20.clone.refs_3_.refs_2_) | copy-start | bytes 1179652
  11.0 23.3 %all-to-all-start = ((f32[64,1,768]{2,1,0:T(1,128)}), f32[64,1,768]{2,1,0:T(1,128)S(1)}, u32[]{:S(2)}, u32[]{:S(2)}) async-start(f32[64,1,768]{2,1,0:T(1,128)} %bitcast.44), calls=%async_computation | async-start | bytes 393216 | tf_op jit(solution)/shard_map/all_to_all | solution.py:362
  23.4 10.9 %copy-start.1 = (f32[2,136,256]{2,1,0:T(8,128)S(1)}, f32[2,136,256]{2,1,0:T(8,128)}, u32[]{:S(2)}) copy-start(f32[2,136,256]{2,1,0:T(8,128)} %constant.21.clone.refs_4_.refs_3_) | copy-start | bytes 835588
  34.3 18.9 %copy-start.3 = (f32[2,136,256]{2,1,0:T(8,128)S(1)}, f32[2,136,256]{2,1,0:T(8,128)}, u32[]{:S(2)}) copy-start(f32[2,136,256]{2,1,0:T(8,128)} %constant.23.clone.refs_2_.refs_4_.refs_5_) | copy-start | bytes 835588
  35.6 17.6 %copy-start.2 = (bf16[640,256]{1,0:T(8,128)(2,1)S(1)}, bf16[640,256]{1,0:T(8,128)(2,1)}, u32[]{:S(2)}) copy-start(bf16[640,256]{1,0:T(8,128)(2,1)} %constant.22.clone.refs_1_.refs_3_.refs_4_) | copy-start | bytes 983044
  175.7 4.7 %collective-permute-start.3 = (f32[2,16,1024]{2,1,0:T(8,128)S(1)}, f32[2,16,1024]{2,1,0:T(8,128)S(1)}, u32[]{:S(2)}, u32[]{:S(2)}) collective-permute-start(f32[2,16,1024]{2,1,0:T(8,128)S(1)} %get-tuple-element.50), channel_id=1, source_target_pairs={{0,64},{64,0},{128,192},{192,128},{1,65},{65,1},{129,193},{193,129... | collective-permute-start | bytes 393224 | tf_op jit(solution)/shard_map/ppermute | solution.py:485

commit v6 on v5

--- a/solution.py
+++ b/solution.py
@@ -406,30 +406,30 @@
         psi = propagate("y", parts_of(value), tab, False)
         outs[0][...] = jnp.concatenate(psi, axis=1)
         a = propagate("y", mul(psi, parts_of(value, 2 * L)), tab, False)
-        put(outs[1], jnp.concatenate(a, axis=1))
+        put(outs[1], jnp.concatenate(a + (ins[1][...],), axis=1))
 
     got2 = exchange(sent)
-    psi1, sent = call(third, "y", (got2,), ((B, 2 * L), (4 * B, 128)))
+    psi1, sent = call(third, "y", (got2, obj[3]), ((B, 2 * L), (8 * B, 128)))
 
     def fourth(tab, ins, outs):
         psi = propagate("x", parts_of(wide(ins[0])), tab, False)
         outs[0][...] = jnp.concatenate(psi, axis=1)
         a = propagate("x", mul(psi, parts_of(ins[1][...])), tab, False)
-        put(outs[1], jnp.concatenate(a + (ins[2][...],), axis=1))
-
+        put(outs[1], jnp.concatenate(a, axis=1))
+
+    got3 = exchange(sent)
     psi2, sent = call(
-        fourth, "x", (exchange(sent), obj[2], obj[3]), ((B, 2 * L), (8 * B, 128))
+        fourth, "x", (got3, obj[2]), ((B, 2 * L), (4 * B, 128))
     )
 
     def fifth(tab, ins, outs):
         value = wide(ins[0])
         psi = propagate("y", parts_of(value), tab, False)
         outs[0][...] = jnp.concatenate(psi, axis=1)
-        a = y_forward(mul(psi, parts_of(value, 2 * L)), tab)
+        a = y_forward(mul(psi, parts_of(wide(ins[1]), 2 * L)), tab)
         put(outs[1], jnp.concatenate(a, axis=1))
 
-    got4 = exchange(sent)
-    psi3, sent = call(fifth, "y", (got4,), ((B, 2 * L), (4 * B, 128)))
+    psi3, sent = call(fifth, "y", (exchange(sent), got3), ((B, 2 * L), (4 * B, 128)))
 
     def far(tab, ins, outs):
         phi = x_forward(parts_of(wide(ins[0])), tab)
@@ -447,7 +447,7 @@
         outs[1][...] = jnp.concatenate(grad, axis=1)
 
     square = ((4 * B, 128), (B, 2 * L))
-    sent, grad3 = call(back_third, "y", (exchange(sent), psi3, got4), square)
+    sent, grad3 = call(back_third, "y", (exchange(sent), psi3, got3), square)
 
     def back_second(tab, ins, outs):
         adj = propagate("x", parts_of(wide(ins[0])), tab, True)

time: 182 us -> 182 us (level)
  no operation moved by 1% of the time
where the time goes in v6:
time: 182 us; the launch traced here: 181 us
  blocking collectives  128 us (70%)
  starting transfers between devices  19.7 us (11%)
  Pallas kernels  19 us (10%)
  waiting for transfers between devices  13.1 us (7%)
    all_to_all x8, blocking collectives, exchange(): return lax.all_to_all(value, 'row', split_axis=0, concat_axis=0, tiled=True)  128 us
    pallas_call x11, Pallas kernels, call(): pl.pallas_call(kernel, out_shape=[jax.ShapeDtypeStruct(shape, f32) for sh...  15.4 us
    all_to_all x1, starting transfers between devices, exchange(): return lax.all_to_all(value, 'row', split_axis=0, concat_axis=0, tiled=True)  12.4 us
    all_to_all x1, waiting for transfers between devices, exchange(): return lax.all_to_all(value, 'row', split_axis=0, concat_axis=0, tiled=True)  8.78 us
    ppermute x3, starting transfers between devices, moved(): return lax.ppermute(own, 'section', [(s, (s + k) % 4) for s in range(4)])  6.25 us
  transfers between devices with their start and end apart: 5, of which 3 were waited for; matrix products, arithmetic and copies ran while one was open for 0% of the time, Pallas kernels for 3%

profile of v6, /device:TPU:1, one launch (start us, length us, event | category | flops | bytes accessed | tf_op | source)
XLA Modules:
  0.0 181.1 jit_solution(4008370912081970215)
XLA Ops:
  0.0 3.6 %collective-permute-start.2 = (f32[2,16,1024]{2,1,0:T(8,128)}, f32[2,16,1024]{2,1,0:T(8,128)S(1)}, u32[]{:S(2)}, u32[]{:S(2)}) collective-permute-start(f32[2,16,1024]{2,1,0:T(8,128)} %bitcast.41), channel_id=1, source_target_pairs={{0,128},{64,192},{128,0},{192,64},{1,129},{65,193},{129,1},{193,65... | collective-permute-start | bytes 393224 | tf_op jit(solution)/shard_map/ppermute | solution.py:368
  3.6 0.3 collective-permute-start.1
  3.9 2.4 %collective-permute-start = (f32[2,16,1024]{2,1,0:T(8,128)}, f32[2,16,1024]{2,1,0:T(8,128)S(1)}, u32[]{:S(2)}, u32[]{:S(2)}) collective-permute-start(f32[2,16,1024]{2,1,0:T(8,128)} %bitcast.43), channel_id=1, source_target_pairs={{0,192},{64,0},{128,64},{192,128},{1,193},{65,1},{129,65},{193,129... | collective-permute-start | bytes 393224 | tf_op jit(solution)/shard_map/ppermute | solution.py:368
  6.3 0.0 copy-start.4
  6.3 3.5 %shard_map.118 = f32[384,128]{1,0:T(8,128)} custom-call(s32[2,2]{1,0:T(2,128)} %offsets_ref.1, f32[2,16,1024]{2,1,0:T(8,128)} %probe_ref.1, f32[2,16,1024]{2,1,0:T(8,128)} %target_ref.1, bf16[128,192]{1,0:T(8,128)(2,1)} %constant.16.clone.ly, bf16[256,256]{1,0:T(8,128)(2,1)} %constant.17.clone.pm, f32[2,72,256]{2,1,0:T(8,128)} %constant.18.clone.small, ...), custom_call_target="tpu_custom_call" | custom-call | tf_op jit(solution)/shard_map/pallas_call | solution.py:350
  9.8 0.0 collective-permute-done.2.refs_2_
  9.8 1.2 collective-permute-done.1.refs_1_
  11.0 0.0 collective-permute-done.refs_3_
  11.0 0.0 copy-start
  11.0 12.4 %all-to-all-start = ((f32[64,1,768]{2,1,0:T(1,128)}), f32[64,1,768]{2,1,0:T(1,128)S(1)}, u32[]{:S(2)}, u32[]{:S(2)}) async-start(f32[64,1,768]{2,1,0:T(1,128)} %bitcast.45), calls=%async_computation | async-start | bytes 393216 | tf_op jit(solution)/shard_map/all_to_all | solution.py:362
  23.4 0.0 copy-done.4
  23.4 0.0 copy-start.1
  23.4 2.1 %shard_map.119 = (f32[64,512]{1,0:T(8,128)S(1)}, f32[64,512]{1,0:T(8,128)S(1)}, f32[64,512]{1,0:T(8,128)S(1)}, f32[64,512]{1,0:T(8,128)S(1)}) custom-call(f32[2,16,1024]{2,1,0:T(8,128)S(1)} %bitcast.44, f32[2,16,1024]{2,1,0:T(8,128)S(1)} %collective-permute-done.1.refs_1_, f32[2,16,1024]{2,1,0:T(8,128)S(1)} %collective-permute-done.2.refs_2_, ...), custom_call_target="tpu_custom_call" | custom-call | tf_op jit(solution)/shard_map/pallas_call | solution.py:319
  25.6 8.8 %all-to-all-done = f32[64,1,768]{2,1,0:T(1,128)S(1)} async-done(((f32[64,1,768]{2,1,0:T(1,128)}), f32[64,1,768]{2,1,0:T(1,128)S(1)}, u32[]{:S(2)}, u32[]{:S(2)}) %all-to-all-start) | async-done | bytes 196640 | tf_op jit(solution)/shard_map/all_to_all | solution.py:362
  34.3 0.0 copy-done
  34.3 0.0 copy-done.1
  34.3 0.0 copy-start.3
  34.3 1.3 shard_map.120
  35.6 0.0 copy-start.2
  35.6 17.6 %all_to_all.93 = f32[64,8,128]{2,1,0:T(8,128)S(1)} all-to-all(f32[64,8,128]{2,1,0:T(8,128)S(1)} %bitcast.35), channel_id=1, replica_groups=mesh['section'=4,'row'=64] {'row'}, dimensions={0} | all-to-all | bytes 524288 | tf_op jit(solution)/shard_map/all_to_all | solution.py:362
  53.3 0.0 copy-done.3
  53.3 0.0 copy-done.2
  53.3 1.7 shard_map.121
  54.9 17.8 %all_to_all.94 = f32[64,8,128]{2,1,0:T(8,128)S(1)} all-to-all(f32[64,8,128]{2,1,0:T(8,128)S(1)} %bitcast.36), channel_id=1, replica_groups=mesh['section'=4,'row'=64] {'row'}, dimensions={0} | all-to-all | bytes 524288 | tf_op jit(solution)/shard_map/all_to_all | solution.py:362
  72.8 1.7 shard_map.122
  74.5 16.2 %all_to_all.95 = f32[64,4,128]{2,1,0:T(4,128)S(1)} all-to-all(f32[64,4,128]{2,1,0:T(4,128)S(1)} %bitcast.40), channel_id=1, replica_groups=mesh['section'=4,'row'=64] {'row'}, dimensions={0} | all-to-all | bytes 262144 | tf_op jit(solution)/shard_map/all_to_all | solution.py:362
  90.7 1.2 shard_map.123
  91.9 15.0 %all_to_all.96 = f32[64,4,128]{2,1,0:T(4,128)S(1)} all-to-all(f32[64,4,128]{2,1,0:T(4,128)S(1)} %bitcast.39), channel_id=1, replica_groups=mesh['section'=4,'row'=64] {'row'}, dimensions={0} | all-to-all | bytes 262144 | tf_op jit(solution)/shard_map/all_to_all | solution.py:362
  106.9 0.9 shard_map.124
  107.8 15.0 %all_to_all.97 = f32[64,4,128]{2,1,0:T(4,128)S(1)} all-to-all(f32[64,4,128]{2,1,0:T(4,128)S(1)} %bitcast.33), channel_id=1, replica_groups=mesh['section'=4,'row'=64] {'row'}, dimensions={0} | all-to-all | bytes 262144 | tf_op jit(solution)/shard_map/all_to_all | solution.py:362
  122.8 1.3 shard_map.125
  124.1 15.0 %all_to_all.98 = f32[64,4,128]{2,1,0:T(4,128)S(1)} all-to-all(f32[64,4,128]{2,1,0:T(4,128)S(1)} %bitcast.37), channel_id=1, replica_groups=mesh['section'=4,'row'=64] {'row'}, dimensions={0} | all-to-all | bytes 262144 | tf_op jit(solution)/shard_map/all_to_all | solution.py:362
  139.2 1.7 shard_map.126
  140.9 15.0 %all_to_all.99 = f32[64,4,128]{2,1,0:T(4,128)S(1)} all-to-all(f32[64,4,128]{2,1,0:T(4,128)S(1)} %bitcast.38), channel_id=1, replica_groups=mesh['section'=4,'row'=64] {'row'}, dimensions={0} | all-to-all | bytes 262144 | tf_op jit(solution)/shard_map/all_to_all | solution.py:362
  155.9 1.7 shard_map.127
  157.6 16.7 %all_to_all.100 = f32[64,8,128]{2,1,0:T(8,128)S(1)} all-to-all(f32[64,8,128]{2,1,0:T(8,128)S(1)} %bitcast.27), channel_id=1, replica_groups=mesh['section'=4,'row'=64] {'row'}, dimensions={0} | all-to-all | bytes 524288 | tf_op jit(solution)/shard_map/all_to_all | solution.py:362
  174.3 1.4 shard_map.128
  175.7 1.0 collective-permute-start.3
  176.7 0.6 shard_map.129
  177.3 3.1 %collective-permute-done.3 = f32[2,16,1024]{2,1,0:T(8,128)S(1)} collective-permute-done((f32[2,16,1024]{2,1,0:T(8,128)S(1)}, f32[2,16,1024]{2,1,0:T(8,128)S(1)}, u32[]{:S(2)}, u32[]{:S(2)}) %collective-permute-start.3) | collective-permute-done | bytes 131104 | tf_op jit(solution)/shard_map/ppermute | solution.py:485
  180.4 0.7 add_bitcast_fusion
Async XLA Ops:
  0.0 9.8 %collective-permute-start.2 = (f32[2,16,1024]{2,1,0:T(8,128)}, f32[2,16,1024]{2,1,0:T(8,128)S(1)}, u32[]{:S(2)}, u32[]{:S(2)}) collective-permute-start(f32[2,16,1024]{2,1,0:T(8,128)} %bitcast.41), channel_id=1, source_target_pairs={{0,128},{64,192},{128,0},{192,64},{1,129},{65,193},{129,1},{193,65... | collective-permute-start | bytes 393224 | tf_op jit(solution)/shard_map/ppermute | solution.py:368
  3.6 7.4 %collective-permute-start.1 = (f32[2,16,1024]{2,1,0:T(8,128)}, f32[2,16,1024]{2,1,0:T(8,128)S(1)}, u32[]{:S(2)}, u32[]{:S(2)}) collective-permute-start(f32[2,16,1024]{2,1,0:T(8,128)} %bitcast.42), channel_id=1, source_target_pairs={{0,64},{64,128},{128,192},{192,0},{1,65},{65,129},{129,193},{193,1... | collective-permute-start | bytes 393224 | tf_op jit(solution)/shard_map/ppermute | solution.py:368
  3.9 7.1 %collective-permute-start = (f32[2,16,1024]{2,1,0:T(8,128)}, f32[2,16,1024]{2,1,0:T(8,128)S(1)}, u32[]{:S(2)}, u32[]{:S(2)}) collective-permute-start(f32[2,16,1024]{2,1,0:T(8,128)} %bitcast.43), channel_id=1, source_target_pairs={{0,192},{64,0},{128,64},{192,128},{1,193},{65,1},{129,65},{193,129... | collective-permute-start | bytes 393224 | tf_op jit(solution)/shard_map/ppermute | solution.py:368
  6.3 17.2 %copy-start.4 = (f32[1,2,16,1024]{3,2,1,0:T(8,128)S(1)}, f32[1,2,16,1024]{3,2,1,0:T(8,128)}, u32[]{:S(2)}) copy-start(f32[1,2,16,1024]{3,2,1,0:T(8,128)} %param.12) | copy-start | bytes 393220
  11.0 23.3 %copy-start = (bf16[768,256]{1,0:T(8,128)(2,1)S(1)}, bf16[768,256]{1,0:T(8,128)(2,1)}, u32[]{:S(2)}) copy-start(bf16[768,256]{1,0:T(8,128)(2,1)} %constant.20.clone.refs_3_.refs_2_) | copy-start | bytes 1179652
  11.0 23.3 %all-to-all-start = ((f32[64,1,768]{2,1,0:T(1,128)}), f32[64,1,768]{2,1,0:T(1,128)S(1)}, u32[]{:S(2)}, u32[]{:S(2)}) async-start(f32[64,1,768]{2,1,0:T(1,128)} %bitcast.45), calls=%async_computation | async-start | bytes 393216 | tf_op jit(solution)/shard_map/all_to_all | solution.py:362
  23.4 10.9 %copy-start.1 = (f32[2,136,256]{2,1,0:T(8,128)S(1)}, f32[2,136,256]{2,1,0:T(8,128)}, u32[]{:S(2)}) copy-start(f32[2,136,256]{2,1,0:T(8,128)} %constant.21.clone.refs_4_.refs_3_) | copy-start | bytes 835588
  34.3 18.9 %copy-start.3 = (f32[2,136,256]{2,1,0:T(8,128)S(1)}, f32[2,136,256]{2,1,0:T(8,128)}, u32[]{:S(2)}) copy-start(f32[2,136,256]{2,1,0:T(8,128)} %constant.23.clone.refs_3_.refs_4_.refs_5_) | copy-start | bytes 835588
  35.6 17.6 %copy-start.2 = (bf16[640,256]{1,0:T(8,128)(2,1)S(1)}, bf16[640,256]{1,0:T(8,128)(2,1)}, u32[]{:S(2)}) copy-start(bf16[640,256]{1,0:T(8,128)(2,1)} %constant.22.clone.refs_2_.refs_3_.refs_4_) | copy-start | bytes 983044
  175.7 4.7 %collective-permute-start.3 = (f32[2,16,1024]{2,1,0:T(8,128)S(1)}, f32[2,16,1024]{2,1,0:T(8,128)S(1)}, u32[]{:S(2)}, u32[]{:S(2)}) collective-permute-start(f32[2,16,1024]{2,1,0:T(8,128)S(1)} %get-tuple-element.50), channel_id=1, source_target_pairs={{0,64},{64,0},{128,192},{192,128},{1,65},{65,1},{129,193},{193,129... | collective-permute-start | bytes 393224 | tf_op jit(solution)/shard_map/ppermute | solution.py:485
